TPU v7x, 256 devices: a whole 4x4x8 slice. The times are simulated.
256 devices in a mesh: rep: 2 (over core), ep: 128 (over x, z, y).
Axes of the slice: x: 4, y: 4, z: 8, core: 2. Of those that a mesh axis runs over, the one named last changes fastest.
Arguments:
- first_half: bfloat16 [16384, 2048], P('ep'), may hold values from -6 to 6
- second_half: bfloat16 [16384, 2048], P('ep'), may hold values from -6 to 6
- second_grad: bfloat16 [16384, 2048], P('ep'), may hold values from -3 to 3
- norm_gain: bfloat16 [2048], replicated, may hold values from 0.5 to 1.5
- expert_ids: int32 [16384, 8], P('ep'), may hold values from 0 to 127, all different within a row; in each aligned block of 128 rows (0 to 127, 128 to 255, ...) at most 10 rows name the same one
- gates: float32 [16384, 8], P('ep'), may hold values from 0.02 to 0.3
- w_gate: bfloat16 [128, 2048, 768], P('ep', None, 'rep'), may hold values from -0.125 to 0.125
- w_up: bfloat16 [128, 2048, 768], P('ep', None, 'rep'), may hold values from -0.125 to 0.125
- w_down: bfloat16 [128, 768, 2048], P('ep', 'rep'), may hold values from -0.21875 to 0.21875
Outputs:
- inverted: bfloat16 [16384, 2048], P('ep')
- first_grad: bfloat16 [16384, 2048], P('ep')
- gates_grad: float32 [16384, 8], P('ep')
- w_down_grad: bfloat16 [128, 768, 2048], P('ep', 'rep')
Inputs may be any that keep to these rules, and one draw needn't show every extreme that they name: `expert_ids`: the 8 experts of a token are different. Among the tokens of one index of ep (aligned blocks of 128 rows) no expert is named by more than 10 tokens, and in every draw some expert is named by exactly 10 tokens of some block.
All inputs are finite; a program needn't handle non-finite values.
Results may differ from a plain program's by a relative error of at most 0.0072.
Values may be sent and summed in bfloat16 or wider, within the bound.
A program may use at most 128 MiB of HBM per device.

v0:
```python
import jax
import jax.numpy as jnp
from jax import lax
from jax.sharding import PartitionSpec as P

EPSILON = 1e-06


def contract_rows(left, right):
    return lax.dot_general(
        left, right, (((0,), (0,)), ((), ())), preferred_element_type=jnp.float32
    )


def contract_cols(left, right):
    return lax.dot_general(
        left, right, (((1,), (1,)), ((), ())), preferred_element_type=jnp.float32
    )


def expert_pass(row_inputs, row_scaled, gate_mat, up_mat, down_mat):
    gate_pre = jnp.dot(row_inputs, gate_mat, preferred_element_type=jnp.float32)
    up_pre = jnp.dot(row_inputs, up_mat, preferred_element_type=jnp.float32)
    sigmoid_gate = jax.nn.sigmoid(gate_pre)
    swish_gate = gate_pre * sigmoid_gate
    hidden = (swish_gate * up_pre).astype(jnp.bfloat16)
    output = jnp.dot(hidden, down_mat, preferred_element_type=jnp.float32)
    hidden_grad = contract_cols(row_scaled, down_mat)
    gate_grad = (
        hidden_grad * up_pre * sigmoid_gate * (1.0 + gate_pre * (1.0 - sigmoid_gate))
    ).astype(jnp.bfloat16)
    up_grad = (hidden_grad * swish_gate).astype(jnp.bfloat16)
    input_grad = contract_cols(gate_grad, gate_mat) + contract_cols(up_grad, up_mat)
    return (output, input_grad, contract_rows(hidden, row_scaled))


def local(first_half, second_half, second_grad, norm_gain, expert_ids, gates, w_gate, w_up, w_down):
    token_count, model_width = first_half.shape
    top_count = expert_ids.shape[1]
    local_experts = w_gate.shape[0]
    owners = lax.axis_size("ep")
    replicas = lax.axis_size("rep")
    replica_index = lax.axis_index("rep")
    experts_all = local_experts * owners
    assigned = token_count * top_count
    capacity = 5 * token_count * top_count // (4 * experts_all)
    portion = capacity // replicas
    slots_all = experts_all * capacity
    slots_mine = experts_all * portion
    full_gate, full_up, full_down = (
        lax.all_gather(w_gate, "rep", axis=2, tiled=True),
        lax.all_gather(w_up, "rep", axis=2, tiled=True),
        lax.all_gather(w_down, "rep", axis=1, tiled=True),
    )
    expert_range = jnp.arange(experts_all, dtype=jnp.int32)
    hits = (expert_ids[:, :, None] == expert_range[None, None, :]).astype(jnp.bfloat16)
    incidence = jnp.sum(hits, axis=1)
    token_range = jnp.arange(token_count, dtype=jnp.int32)
    strictly_before = (token_range[:, None] > token_range[None, :]).astype(jnp.bfloat16)
    earlier = jnp.dot(strictly_before, incidence, preferred_element_type=jnp.float32)
    slot_rank = jnp.sum(hits.astype(jnp.float32) * earlier[:, None, :], axis=2).astype(jnp.int32)
    flat_ids = expert_ids.reshape(assigned)
    flat_rank = slot_rank.reshape(assigned)
    target = flat_ids * capacity + flat_rank
    local_rank = flat_rank - replica_index * portion
    is_mine = (local_rank >= 0) & (local_rank < portion)
    destination = jnp.where(is_mine, flat_ids * portion + local_rank, slots_mine)
    slot_source = (
        jnp.full((slots_mine,), assigned, jnp.int32)
        .at[destination]
        .set(jnp.arange(assigned, dtype=jnp.int32), mode="drop")
    )
    is_live = slot_source < assigned
    clamped = jnp.minimum(slot_source, assigned - 1)
    source_token = clamped // top_count
    values = first_half.astype(jnp.float32)
    inverse = lax.rsqrt(jnp.mean(values * values, axis=1, keepdims=True) + EPSILON)
    gain_value = norm_gain.astype(jnp.float32)
    normed = (values * inverse * gain_value).astype(jnp.bfloat16)
    flat_gates = gates.reshape(assigned)
    zero_half = jnp.zeros((), jnp.bfloat16)
    mine_inputs = jnp.where(is_live[:, None], normed[source_token], zero_half)
    slot_scaled = (
        flat_gates[clamped][:, None] * second_grad[source_token].astype(jnp.float32)
    ).astype(jnp.bfloat16)
    mine_scaled = jnp.where(is_live[:, None], slot_scaled, zero_half)
    got_inputs, got_scaled = (
        lax.all_to_all(mine_inputs, "ep", split_axis=0, concat_axis=0, tiled=True),
        lax.all_to_all(mine_scaled, "ep", split_axis=0, concat_axis=0, tiled=True),
    )
    grouped_inputs = got_inputs.reshape(owners, local_experts, portion, model_width)
    grouped_scaled = got_scaled.reshape(owners, local_experts, portion, model_width)
    out_list, grad_list, down_list = ([], [], [])
    row_inputs = grouped_inputs[:, 0].reshape(owners * portion, model_width)
    row_scaled = grouped_scaled[:, 0].reshape(owners * portion, model_width)
    output, input_grad, grad_down = expert_pass(
        row_inputs, row_scaled, full_gate[0], full_up[0], full_down[0]
    )
    out_list.append(output.astype(jnp.bfloat16).reshape(owners, 1, portion, model_width))
    grad_list.append(input_grad.astype(jnp.bfloat16).reshape(owners, 1, portion, model_width))
    down_list.append(grad_down)
    back_out = out_list[0].reshape(owners * local_experts * portion, model_width)
    back_grad = grad_list[0].reshape(owners * local_experts * portion, model_width)
    summed_down = lax.psum_scatter(jnp.stack(down_list), "rep", scatter_dimension=1, tiled=True)
    w_down_grad = summed_down.astype(jnp.bfloat16)
    returned_out, returned_grad = (
        lax.all_to_all(back_out, "ep", split_axis=0, concat_axis=0, tiled=True),
        lax.all_to_all(back_grad, "ep", split_axis=0, concat_axis=0, tiled=True),
    )
    whole_out, whole_grad = (
        lax.all_gather(
            returned_out.reshape(experts_all, portion, model_width), "rep", axis=1, tiled=True
        ),
        lax.all_gather(
            returned_grad.reshape(experts_all, portion, model_width), "rep", axis=1, tiled=True
        ),
    )
    whole_out = whole_out.reshape(slots_all, model_width)
    whole_grad = whole_grad.reshape(slots_all, model_width)
    out_rows = whole_out[target].reshape(token_count, top_count, model_width)
    grad_rows = whole_grad[target].reshape(token_count, top_count, model_width)
    inverted = (
        second_half.astype(jnp.float32)
        - jnp.sum(gates[:, :, None] * out_rows.astype(jnp.float32), axis=1)
    ).astype(jnp.bfloat16)
    gates_grad = jnp.einsum("td,tkd->tk", second_grad, out_rows, preferred_element_type=jnp.float32)
    normed_grad = jnp.sum(grad_rows.astype(jnp.float32), axis=1) * gain_value
    first_grad = (
        inverse * normed_grad
        - values
        * inverse
        * inverse
        * inverse
        * jnp.mean(normed_grad * values, axis=1, keepdims=True)
    ).astype(jnp.bfloat16)
    return (inverted, first_grad, gates_grad, w_down_grad)


def solution(mesh):
    return jax.shard_map(
        local,
        mesh=mesh,
        in_specs=(
            P("ep", None),
            P("ep", None),
            P("ep", None),
            P(),
            P("ep", None),
            P("ep", None),
            P("ep", None, "rep"),
            P("ep", None, "rep"),
            P("ep", "rep", None),
        ),
        out_specs=(P("ep", None), P("ep", None), P("ep", None), P("ep", "rep", None)),
        check_vma=False,
    )
```

profile of v0, /device:TPU:1, one launch (start us, length us, event | category | flops | bytes accessed | tf_op | source)
XLA Modules:
  0.0 615.5 jit_solution(16634717604469102683)
XLA Ops:
  9.8 4.3 scatter_custom_fusion
  17.3 4.1 gather_fusion
  21.4 5.4 gather.18
  26.8 3.4 gather_fusion.3
  30.2 3.7 reshape.167
  37.4 7.7 %fusion = (bf16[128,5,2048]{2,1,0:T(8,128)(2,1)}, bf16[128,5,2048]{2,1,0:T(8,128)(2,1)}) fusion(f32[128,5,2048]{2,1,0:T(8,128)} %reshape.167, f32[128,5]{1,0:T(8,128)S(1)} %mul.149, pred[128,5]{1,0:T(8,128)(4,1)S(1)} %broadcast_in_dim.27, bf16[128,5,2048]{2,1,0:T(8,128)(2,1)} %gather.18), kind=kLoop, calls=%fused_computation.10 | loop fusion | flops 5242880 | bytes 13110400 | tf_op jit(solution)/shard_map/jit(_where)/select_n | solution.py:86
  45.1 16.9 %all-to-all-start = ((bf16[128,5,2048]{2,1,0:T(8,128)(2,1)}), bf16[128,5,2048]{2,1,0:T(8,128)(2,1)}, u32[]{:S(2)}, u32[]{:S(2)}) async-start(bf16[128,5,2048]{2,1,0:T(8,128)(2,1)} %get-tuple-element.5), calls=%async_computation | async-start | bytes 8388608 | tf_op jit(solution)/shard_map/all_to_all | solution.py:88
  62.7 92.0 %all-to-all-done = bf16[128,5,2048]{2,1,0:T(8,128)(2,1)} async-done(((bf16[128,5,2048]{2,1,0:T(8,128)(2,1)}), bf16[128,5,2048]{2,1,0:T(8,128)(2,1)}, u32[]{:S(2)}, u32[]{:S(2)}) %all-to-all-start) | async-done | bytes 2621472 | tf_op jit(solution)/shard_map/all_to_all | solution.py:88
  154.7 11.2 %all-to-all-start.2 = ((bf16[128,5,2048]{2,1,0:T(8,128)(2,1)}), bf16[128,5,2048]{2,1,0:T(8,128)(2,1)}, u32[]{:S(2)}, u32[]{:S(2)}) async-start(bf16[128,5,2048]{2,1,0:T(8,128)(2,1)} %get-tuple-element.4), calls=%async_computation.2 | async-start | bytes 8388608 | tf_op jit(solution)/shard_map/all_to_all | solution.py:89
  167.9 5.6 all_to_all.25
  173.5 85.0 %all-to-all-done.2 = bf16[128,5,2048]{2,1,0:T(8,128)(2,1)} async-done(((bf16[128,5,2048]{2,1,0:T(8,128)(2,1)}), bf16[128,5,2048]{2,1,0:T(8,128)(2,1)}, u32[]{:S(2)}, u32[]{:S(2)}) %all-to-all-start.2) | async-done | bytes 2621472 | tf_op jit(solution)/shard_map/all_to_all | solution.py:89
  258.5 4.2 all_to_all.29
  262.7 6.2 %fusion.11 = f32[640,768]{1,0:T(8,128)} fusion(bf16[640,2048]{1,0:T(8,128)(2,1)} %all_to_all.25, bf16[1,2048,768]{2,1,0:T(8,128)(2,1)} %all-gather.6.cloned.1.call-done), kind=kOutput, calls=%fused_computation.24 | convolution fusion | flops 2013265920 | bytes 7733248 | tf_op jit(solution)/shard_map/dot_general | solution.py:22
  268.8 7.1 %multiply_convert_fusion.3 = (bf16[640,768]{1,0:T(8,128)(2,1)}, f32[640,768]{1,0:T(8,128)}) fusion(f32[640,768]{1,0:T(8,128)} %fusion.11, bf16[640,2048]{1,0:T(8,128)(2,1)} %all_to_all.25, bf16[1,2048,768]{2,1,0:T(8,128)(2,1)} %all-gather.8.cloned.1.call-done), kind=kOutput, calls=%fused_computation.28 | convolution fusion | flops 2016215040 | bytes 10682368 | tf_op jit(solution)/shard_map/dot_general | solution.py:23
  276.0 4.3 fusion.3
  283.1 3.8 add_convert_fusion
  286.9 5.4 all_to_all.30
  292.3 103.9 %all_to_all.36 = bf16[128,5,2048]{2,1,0:T(8,128)(2,1)S(1)} all-to-all(bf16[128,5,2048]{2,1,0:T(8,128)(2,1)} %all_to_all.30), channel_id=1, replica_groups=mesh['rep'=2,'ep'=128] {'ep'}, dimensions={0} | all-to-all | bytes 5242880 | tf_op jit(solution)/shard_map/all_to_all | solution.py:108
  399.5 6.0 convolution_convert_fusion
  405.5 5.5 all_to_all.26
  410.9 103.3 %all_to_all.37 = bf16[128,5,2048]{2,1,0:T(8,128)(2,1)S(1)} all-to-all(bf16[128,5,2048]{2,1,0:T(8,128)(2,1)} %all_to_all.26), channel_id=1, replica_groups=mesh['rep'=2,'ep'=128] {'ep'}, dimensions={0} | all-to-all | bytes 5242880 | tf_op jit(solution)/shard_map/all_to_all | solution.py:107
  514.2 3.3 copy.44
  517.8 5.7 convolution_bitcast_fusion
  523.8 9.9 %copy.49 = bf16[128,10,2048]{2,1,0:T(8,128)(2,1)} copy(bf16[128,10,2048]{2,0,1:T(8,128)(2,1)} %all-gather.14.cloned.1.call-done) | data formatting | bytes 10485760 | tf_op jit(solution)/shard_map/all_gather | solution.py:114
  533.8 10.0 %reshape.164 = bf16[1280,2048]{1,0:T(8,128)(2,1)} reshape(bf16[128,10,2048]{2,1,0:T(8,128)(2,1)} %copy.49) | data formatting | bytes 10485760 | tf_op jit(solution)/shard_map/reshape | solution.py:119
  543.7 9.1 %copy.45 = bf16[128,10,2048]{2,1,0:T(8,128)(2,1)} copy(bf16[128,10,2048]{2,0,1:T(8,128)(2,1)} %all-gather.12.cloned.1.call-done) | data formatting | bytes 10485760 | tf_op jit(solution)/shard_map/all_gather | solution.py:111
  552.8 10.4 %reshape.161 = bf16[1280,2048]{1,0:T(8,128)(2,1)} reshape(bf16[128,10,2048]{2,1,0:T(8,128)(2,1)} %copy.45) | data formatting | bytes 10485760 | tf_op jit(solution)/shard_map/reshape | solution.py:118
  563.2 12.0 %gather_fusion.4 = bf16[1024,2048]{1,0:T(8,128)(2,1)} fusion(bf16[1280,2048]{1,0:T(8,128)(2,1)} %reshape.164, s32[1024]{0:T(1024)S(1)} %broadcast_clamp_fusion), kind=kCustom, calls=%fused_computation.4 | custom fusion | bytes 8392704 | tf_op jit(solution)/shard_map/gather | solution.py:121
  575.2 12.2 %gather_fusion.1 = bf16[1024,2048]{1,0:T(8,128)(2,1)} fusion(bf16[1280,2048]{1,0:T(8,128)(2,1)} %reshape.161, s32[1024]{0:T(1024)S(1)} %broadcast_clamp_fusion), kind=kCustom, calls=%fused_computation.1 | custom fusion | bytes 8392704 | tf_op jit(solution)/shard_map/gather | solution.py:120
  587.5 4.9 fusion.1
  593.0 5.2 convert_reduce_fusion
  598.5 4.4 multiply_reduce_fusion
  (70 shorter events, 24.7 us)
Async XLA Ops:
  7.2 19.7 %copy-start = (bf16[128,2048]{1,0:T(8,128)(2,1)S(1)}, bf16[128,2048]{1,0:T(8,128)(2,1)}, u32[]{:S(2)}) copy-start(bf16[128,2048]{1,0:T(8,128)(2,1)} %param.11) | copy-start | bytes 1572868
  30.2 3.7 copy-start.4
  45.1 109.6 %all-to-all-start = ((bf16[128,5,2048]{2,1,0:T(8,128)(2,1)}), bf16[128,5,2048]{2,1,0:T(8,128)(2,1)}, u32[]{:S(2)}, u32[]{:S(2)}) async-start(bf16[128,5,2048]{2,1,0:T(8,128)(2,1)} %get-tuple-element.5), calls=%async_computation | async-start | bytes 8388608 | tf_op jit(solution)/shard_map/all_to_all | solution.py:88
  62.0 200.7 %all-gather.6.cloned.1.call-start = ((), (), s32[]{:S(2)}) async-start(), calls=%async_computation.5 | async-start | bytes 4718592 | tf_op jit(solution)/shard_map/all_gather | solution.py:51
  154.7 103.8 %all-to-all-start.2 = ((bf16[128,5,2048]{2,1,0:T(8,128)(2,1)}), bf16[128,5,2048]{2,1,0:T(8,128)(2,1)}, u32[]{:S(2)}, u32[]{:S(2)}) async-start(bf16[128,5,2048]{2,1,0:T(8,128)(2,1)} %get-tuple-element.4), calls=%async_computation.2 | async-start | bytes 8388608 | tf_op jit(solution)/shard_map/all_to_all | solution.py:89
  165.9 103.0 %all-gather.8.cloned.1.call-start = ((), (), s32[]{:S(2)}) async-start(), calls=%async_computation.6 | async-start | bytes 4718592 | tf_op jit(solution)/shard_map/all_gather | solution.py:52
  166.6 109.3 %all-gather.10.cloned.1.call-start = ((), (), s32[]{:S(2)}) async-start(), calls=%async_computation.7 | async-start | bytes 4718592 | tf_op jit(solution)/shard_map/all_gather | solution.py:53
  167.4 356.5 %all-gather.14.cloned.1.call-start = ((), (), s32[]{:S(2)}) async-start(), calls=%async_computation.9 | async-start | bytes 7864320 | tf_op jit(solution)/shard_map/all_gather | solution.py:114
  275.9 4.3 copy-start.5
  275.9 4.3 copy-start.7
  276.0 4.3 copy-start.8
  280.3 2.8 copy-start.6
  399.4 144.3 %all-gather.12.cloned.1.call-start = ((), (), s32[]{:S(2)}) async-start(), calls=%async_computation.8 | async-start | bytes 7864320 | tf_op jit(solution)/shard_map/all_gather | solution.py:111
  517.5 87.4 %reduce-scatter.2.cloned.1.call-start = ((), (), s32[]{:S(2)}) async-start(), calls=%async_computation.10 | async-start | bytes 9437184 | tf_op jit(solution)/shard_map/reduce_scatter | solution.py:104
  593.0 5.2 copy-start.2
  593.0 5.5 copy-start.1
  598.5 4.4 copy-start.3
Sparse Core Ops, SparseCore 0:
  64.6 19.2 all-gather.5
  168.5 20.0 all-gather.7
  190.4 18.7 all-gather.9
  399.6 20.2 all-gather.13
  517.7 20.5 all-gather.11
  540.7 20.9 reduce-scatter.1
where the time goes:
time: 628 us; the launch traced here: 615 us
  blocking collectives  207 us (33%)
  waiting for transfers between devices  179 us (29%)
  local copies, waits for them, and re-layouts  117 us (19%)
  matrix products  40.9 us (7%)
  starting transfers between devices  29 us (5%)
  other arithmetic  27.4 us (4%)
  between operations  14.8 us (2%)
    all_to_all x1, blocking collectives, local(): lax.all_to_all(back_grad, 'ep', split_axis=0, concat_axis=0, tiled=True)  104 us
    all_to_all x1, blocking collectives, local(): lax.all_to_all(back_out, 'ep', split_axis=0, concat_axis=0, tiled=True)  103 us
    all_to_all x1, waiting for transfers between devices, local(): lax.all_to_all(mine_inputs, 'ep', split_axis=0, concat_axis=0, tiled=True)  92 us
    all_to_all x1, waiting for transfers between devices, local(): lax.all_to_all(mine_scaled, 'ep', split_axis=0, concat_axis=0, tiled=True)  85 us
    all_to_all x1, starting transfers between devices, local(): lax.all_to_all(mine_inputs, 'ep', split_axis=0, concat_axis=0, tiled=True)  16.9 us
  transfers between devices with their start and end apart: 8, of which 2 were waited for; matrix products, arithmetic and copies ran while one was open for 18% of the time, Pallas kernels for 0%

commit v1 on v0

v1 whole, which is shorter than its diff:
```python
import jax
import jax.numpy as jnp
import numpy as np
from jax import lax
from jax.experimental import pallas as pl
from jax.experimental.pallas import tpu as pltpu
from jax.sharding import PartitionSpec as P

EPSILON = 1e-06
MESH = pl.DeviceIdType.MESH
BF = jnp.bfloat16
F32 = jnp.float32

NX, NZ, NY = 4, 8, 4
PLANE = NX * NY
TOK = 128
WIDTH = 2048
FF = 768
HALF = FF // 2
TOP = 8
SHARE = 5
SEG = NZ * SHARE
ROWS = PLANE * SEG
UNITS = 4
FU = WIDTH // UNITS
HU = FU // 2
PARTS = 2
PROWS, PCHIPS = ROWS // PARTS, PLANE // PARTS
PTOK, PBLK = NZ * TOK // PARTS, NZ // PARTS


def nt(left, right):
    return lax.dot_general(left, right, (((1,), (1,)), ((), ())), preferred_element_type=F32)


def tn(left, right):
    return lax.dot_general(left, right, (((0,), (0,)), ((), ())), preferred_element_type=F32)


def nn(left, right):
    return jnp.dot(left, right, preferred_element_type=F32)


def kernel(
    first_ref, second_ref, cot_ref, gain_ref, ids_ref, gates_ref, owner_ref, rank_ref,
    wg_hbm, wu_hbm, wd_hbm,
    inv_ref, fg_ref, gg_ref, wdg_hbm,
    wg, wu, wd, ag, meta, sel, selt, gslot, sgsel, sbuf, drecv, rrecv, acc, hid, ggr, ugr,
    rsrecv, wsend, wrecv, dots, dbuf, drx, ggx, obuf, orecv,
    wl_sem, wss, wrs, ags, agr, sbs, sbr, ms, mr, dss, dsr, rss, rsr, ts, tr, qs, qr,
    wgs, wgr, ds_, dr_, es, er, wos, free,
):
    r = lax.axis_index("rep")
    ep = lax.axis_index("ep")
    x, z, y = ep // (NZ * NY), (ep // NY) % NZ, ep % NY

    def at(dx, dz, dy):
        return {"ep": (((x + dx) % NX) * NZ + (z + dz) % NZ) * NY + (y + dy) % NY}

    sib = {"rep": 1 - r}

    def rc(src, dst, send, recv, dev):
        return pltpu.make_async_remote_copy(
            src_ref=src, dst_ref=dst, send_sem=send, recv_sem=recv,
            device_id=dev, device_id_type=MESH,
        )

    barrier = pltpu.get_barrier_semaphore()
    pl.semaphore_signal(barrier, inc=1, device_id=sib, device_id_type=MESH)

    @pl.loop(1, NZ)
    def _(d):
        pl.semaphore_signal(barrier, inc=1, device_id=at(0, d, 0), device_id_type=MESH)

    @pl.loop(1, PLANE)
    def _(n):
        pl.semaphore_signal(barrier, inc=1, device_id=at(n // NY, 0, n % NY), device_id_type=MESH)

    def local_weights():
        cols = pl.ds(pl.multiple_of(r * HALF, 128), HALF)
        return [
            pltpu.make_async_copy(wg_hbm, wg.at[:, cols], wl_sem.at[0]),
            pltpu.make_async_copy(wu_hbm, wu.at[:, cols], wl_sem.at[1]),
            pltpu.make_async_copy(wd_hbm, wd.at[cols, :], wl_sem.at[2]),
        ]

    def sibling_weights():
        cols = pl.ds(pl.multiple_of(r * HALF, 128), HALF)
        return [
            rc(wg_hbm, wg.at[:, cols], wss.at[0], wrs.at[0], sib),
            rc(wu_hbm, wu.at[:, cols], wss.at[1], wrs.at[1], sib),
            rc(wd_hbm, wd.at[cols, :], wss.at[2], wrs.at[2], sib),
        ]

    for copy in local_weights():
        copy.start()

    values = first_ref[...].astype(F32)
    inverse = lax.rsqrt(jnp.mean(values * values, axis=1, keepdims=True) + EPSILON)
    normed = (values * inverse * gain_ref[...].astype(F32)).astype(BF)
    for u in range(UNITS):
        ag[0, u, 0] = normed[:, u * FU : (u + 1) * FU]
        ag[1, u, 0] = cot_ref[:, u * FU : (u + 1) * FU]
    eye = (
        lax.broadcasted_iota(jnp.int32, (TOK, TOK), 0)
        == lax.broadcasted_iota(jnp.int32, (TOK, TOK), 1)
    ).astype(F32)
    ids_t = lax.dot_general(
        ids_ref[...].astype(F32), eye, (((0,), (0,)), ((), ())),
        preferred_element_type=F32, precision=lax.Precision.HIGHEST,
    )
    meta[0, 0:TOP] = ids_t
    meta[0, TOP : 2 * TOP] = gates_ref[...]

    pl.semaphore_wait(barrier, NZ + PLANE - 1)

    def ag_copy(u, way, step):
        sign = 1 - 2 * way
        src = (NZ - (step - 1)) % NZ if way == 0 else step - 1
        dst = NZ - step if way == 0 else step
        cols = slice(None)
        if step == 4:
            cols = slice(0, HU) if way == 0 else slice(HU, FU)
        return rc(
            ag.at[r, u, src, :, cols], ag.at[r, u, dst, :, cols],
            ags.at[u, way, step - 1], agr.at[u, way, step - 1], at(0, sign, 0),
        )

    def sib_copy(u, j):
        return rc(ag.at[r, u, j], ag.at[r, u, j], sbs.at[u, j], sbr.at[u, j], sib)

    def sib_wait(u, j):
        return rc(ag.at[1 - r, u, j], ag.at[1 - r, u, j], sbs.at[u, j], sbr.at[u, j], sib)

    def ag_first(u):
        ag_copy(u, 0, 1).start()
        ag_copy(u, 1, 1).start()

    def ag_next(u, step):
        for way in range(2):
            ag_copy(u, way, step - 1).wait_recv()
            ag_copy(u, way, step).start()
        for j in (NZ - (step - 1), step - 1):
            sib_copy(u, j).start()

    ag_first(0)

    def meta_copy(d):
        return rc(meta.at[0], meta.at[NZ - d], ms.at[d], mr.at[NZ - d], at(0, d, 0))

    @pl.loop(1, NZ)
    def _(d):
        meta_copy(d).start()

    for copy in sibling_weights():
        copy.start()

    @pl.loop(1, NZ)
    def _(d):
        meta_copy(d).wait_recv()

    d_index = lax.broadcasted_iota(jnp.int32, (PLANE, 1), 0)
    dx, dy = d_index >> 2, d_index & 3
    ex, ey = x + dx, y + dy
    ex = jnp.where(ex >= NX, ex - NX, ex)
    ey = jnp.where(ey >= NY, ey - NY, ey)

    def experts_of(plane):
        return ((ex * NZ + plane) * NY + ey).astype(F32)

    experts = experts_of(z)
    before = (
        lax.broadcasted_iota(jnp.int32, (TOK, TOK), 0)
        < lax.broadcasted_iota(jnp.int32, (TOK, TOK), 1)
    ).astype(BF)
    gslot[...] = jnp.zeros_like(gslot)
    owner = owner_ref[...]
    first_rank = (r * SHARE).astype(F32)
    for j in range(NZ):
        hits = jnp.zeros((PLANE, TOK), F32)
        weight = jnp.zeros((PLANE, TOK), F32)
        for k in range(TOP):
            match = meta[j, k : k + 1, :] == experts
            hits = hits + jnp.where(match, 1.0, 0.0)
            weight = weight + jnp.where(match, meta[j, TOP + k : TOP + k + 1, :], 0.0)
        rank = nn(hits.astype(BF), before)
        rank = jnp.where(hits > 0.0, rank, -1.0)
        slot_rank = nn(owner.astype(BF), rank.astype(BF))
        chosen = jnp.where(slot_rank == rank_ref[:, j : j + 1] + first_rank, 1.0, 0.0)
        slot_gate = jnp.dot(
            owner, weight, preferred_element_type=F32, precision=lax.Precision.HIGHEST
        )
        gslot[...] += jnp.sum(chosen * slot_gate, axis=1, keepdims=True)
        sel[:, j * TOK : (j + 1) * TOK] = chosen.astype(BF)
        selt[j * TOK : (j + 1) * TOK, :] = chosen.T.astype(BF)

    def back(n):
        i, j = n // NY, n % NY
        return ((NX - i) % NX) * NY + (NY - j) % NY

    def disp_copy(u, n):
        m = back(n)
        return rc(sbuf.at[u, n], drecv.at[u, m], dss.at[u, n], dsr.at[u, m], at(n // NY, 0, n % NY))

    def ret_copy(u, n):
        m = back(n)
        return rc(sbuf.at[u, n], rrecv.at[u, m], rss.at[u, n], rsr.at[u, m], at(n // NY, 0, n % NY))

    def select(u):
        @pl.loop(0, PARTS)
        def _(c):
            part = pl.ds(pl.multiple_of(c * PROWS, PROWS), PROWS)
            chips = pl.ds(c * PCHIPS, PCHIPS)
            rows = nn(sel[part, :], ag[0, u].reshape(NZ * TOK, FU)).astype(BF)
            sbuf[u, chips, :, 0:FU] = rows.reshape(PCHIPS, SEG, FU)
            cots = nn(sel[part, :], ag[1, u].reshape(NZ * TOK, FU))
            sgsel[u, part, :] = cots.astype(BF)
            scaled = (cots * gslot[part, :]).astype(BF)
            sbuf[u, chips, :, FU:] = scaled.reshape(PCHIPS, SEG, FU)

        drecv[u, 0] = sbuf[u, 0]

        @pl.loop(1, PLANE)
        def _(n):
            disp_copy(u, n).start()

    @pl.loop(0, UNITS + 1)
    def _(p):
        u = p - 1

        @pl.when((p >= 1) & (p < UNITS))
        def _():
            ag_first(p)

        @pl.when(p >= 1)
        def _():
            ag_next(u, 3)

        @pl.when(p < UNITS)
        def _():
            ag_next(p, 2)

        @pl.when(p >= 1)
        def _():
            ag_next(u, 4)
            ag_copy(u, 0, 4).wait_recv()
            ag_copy(u, 1, 4).wait_recv()
            sib_copy(u, 4).start()
            for j in range(1, NZ):
                sib_wait(u, j).wait_recv()
            select(u)

    @pl.loop(0, UNITS)
    def _(u):
        for step in range(1, 5):
            ag_copy(u, 0, step).wait_send()
            ag_copy(u, 1, step).wait_send()
        for j in range(1, NZ):
            sib_copy(u, j).wait_send()

    pl.semaphore_signal(free, inc=1, device_id=sib, device_id_type=MESH)

    for copy in local_weights():
        copy.wait()
    for copy in sibling_weights():
        copy.wait_send()
    other = pl.ds(pl.multiple_of((1 - r) * HALF, 128), HALF)
    rc(wg_hbm, wg.at[:, other], wss.at[0], wrs.at[0], sib).wait_recv()
    rc(wu_hbm, wu.at[:, other], wss.at[1], wrs.at[1], sib).wait_recv()
    rc(wd_hbm, wd.at[other, :], wss.at[2], wrs.at[2], sib).wait_recv()

    acc[...] = jnp.zeros_like(acc)

    @pl.loop(0, UNITS)
    def _(u):
        @pl.loop(1, PLANE)
        def _(n):
            disp_copy(u, n).wait_recv()

        feats = pl.ds(pl.multiple_of(u * FU, FU), FU)

        @pl.loop(0, PARTS)
        def _(c):
            part = pl.ds(pl.multiple_of(c * PROWS, PROWS), PROWS)
            chips = pl.ds(c * PCHIPS, PCHIPS)
            rows = drecv[u, chips, :, 0:FU].reshape(PROWS, FU)
            acc[0, part, :] += nn(rows, wg[feats, :])
            acc[1, part, :] += nn(rows, wu[feats, :])
            cots = drecv[u, chips, :, FU:].reshape(PROWS, FU)
            acc[2, part, :] += nt(cots, wd[:, feats])

    @pl.loop(0, ROWS // 80)
    def _(c):
        part = pl.ds(pl.multiple_of(c * 80, 16), 80)
        gate_pre, up_pre, grad = acc[0, part, :], acc[1, part, :], acc[2, part, :]
        sig = jax.nn.sigmoid(gate_pre)
        swish = gate_pre * sig
        hid[part, :] = (swish * up_pre).astype(BF)
        ggr[part, :] = (grad * up_pre * sig * (1.0 + gate_pre * (1.0 - sig))).astype(BF)
        ugr[part, :] = (grad * swish).astype(BF)

    @pl.loop(0, UNITS)
    def _(u):
        @pl.loop(1, PLANE)
        def _(n):
            disp_copy(u, n).wait_send()

        feats = pl.ds(pl.multiple_of(u * FU, FU), FU)

        @pl.loop(0, PARTS)
        def _(c):
            part = pl.ds(pl.multiple_of(c * PROWS, PROWS), PROWS)
            chips = pl.ds(c * PCHIPS, PCHIPS)
            outs = nn(hid[part, :], wd[:, feats]).astype(BF)
            sbuf[u, chips, :, 0:FU] = outs.reshape(PCHIPS, SEG, FU)
            grads = (nt(ggr[part, :], wg[feats, :]) + nt(ugr[part, :], wu[feats, :])).astype(BF)
            sbuf[u, chips, :, FU:] = grads.reshape(PCHIPS, SEG, FU)

        rrecv[u, 0] = sbuf[u, 0]

        @pl.loop(1, PLANE)
        def _(n):
            ret_copy(u, n).start()

    def wd_copy(u):
        return rc(wsend.at[u], wrecv.at[u], wgs.at[u], wgr.at[u], sib)

    @pl.loop(0, UNITS)
    def _(u):
        half = hid[:, pl.ds(pl.multiple_of((1 - r) * HALF, 128), HALF)]
        wsend[u] = tn(half, drecv[u, :, :, FU:].reshape(ROWS, FU)).astype(BF)
        wd_copy(u).start()

    def wd_out(u):
        feats = pl.ds(pl.multiple_of(u * FU, FU), FU)
        return pltpu.make_async_copy(wsend.at[u], wdg_hbm.at[:, feats], wos.at[u])

    mine = pl.ds(pl.multiple_of(r * HALF, 128), HALF)

    @pl.loop(0, UNITS)
    def _(u):
        feats = pl.ds(pl.multiple_of(u * FU, FU), FU)
        part = tn(hid[:, mine], drecv[u, :, :, FU:].reshape(ROWS, FU))
        rc(wsend.at[u], wrecv.at[u], wgs.at[u], wgr.at[u], sib).wait_recv()
        wd_copy(u).wait_send()
        wsend[u] = (part + wrecv[u].astype(F32)).astype(BF)
        wd_out(u).start()

    def t_copy(u):
        return rc(ag.at[0, u], ag.at[1, u], ts.at[u], tr.at[u], sib)

    dots[...] = jnp.zeros_like(dots)
    pl.semaphore_wait(free, 1)

    def combine_other(u):
        @pl.loop(1, PLANE)
        def _(n):
            ret_copy(u, n).wait_recv()

        @pl.loop(0, PARTS)
        def _(c):
            part = pl.ds(pl.multiple_of(c * PROWS, PROWS), PROWS)
            chips = pl.ds(c * PCHIPS, PCHIPS)
            outs = rrecv[u, chips, :, 0:FU].astype(F32).reshape(PROWS, FU)
            dots[part, :] += jnp.sum(outs * sgsel[u, part, :].astype(F32), axis=1, keepdims=True)
            rrecv[u, chips, :, 0:FU] = (outs * gslot[part, :]).astype(BF).reshape(PCHIPS, SEG, FU)

        kept = rrecv[u, :, :, pl.ds(pl.multiple_of((1 - r) * FU, FU), FU)].reshape(ROWS, FU)

        @pl.loop(0, PARTS)
        def _(c):
            part = pl.ds(pl.multiple_of(c * PTOK, PTOK), PTOK)
            blocks = pl.ds(c * PBLK, PBLK)
            ag[0, u, blocks] = nn(selt[part, :], kept).astype(BF).reshape(PBLK, TOK, FU)

        t_copy(u).start()

    def combine_mine(u):
        t_copy(u).wait_recv()
        kept = rrecv[u, :, :, pl.ds(pl.multiple_of(r * FU, FU), FU)].reshape(ROWS, FU)

        @pl.loop(0, PARTS)
        def _(c):
            part = pl.ds(pl.multiple_of(c * PTOK, PTOK), PTOK)
            blocks = pl.ds(c * PBLK, PBLK)
            total = nn(selt[part, :], kept).reshape(PBLK, TOK, FU) + ag[1, u, blocks].astype(F32)
            ag[1, u, blocks] = total.astype(BF)

    def rs_copy(u, way, step):
        sign = 1 - 2 * way
        src = 5 - step if way == 0 else step + 3
        cols = slice(None)
        if step == 1:
            cols = slice(0, HU) if way == 0 else slice(HU, FU)
        return rc(
            ag.at[1, u, src, :, cols], rsrecv.at[u, way, step - 1, :, cols],
            qs.at[u, way, step - 1], qr.at[u, way, step - 1], at(0, sign, 0),
        )

    def rs_next(u, step):
        for way in range(2):
            rs_copy(u, way, step - 1).wait_recv()
            src = 5 - step if way == 0 else step + 3
            cols = slice(0, FU)
            if step == 2:
                cols = slice(0, HU) if way == 0 else slice(HU, FU)
            ag[1, u, src, :, cols] = (
                ag[1, u, src, :, cols].astype(F32)
                + rsrecv[u, way, step - 2, :, cols].astype(F32)
            ).astype(BF)
            rs_copy(u, way, step).start()

    def dots_copy(d):
        return rc(dbuf.at[d], drx.at[NZ - d], ds_.at[d], dr_.at[NZ - d], at(0, d, 0))

    @pl.loop(0, UNITS + 3)
    def _(p):
        @pl.when(p < UNITS)
        def _():
            combine_other(p)

        @pl.when((p >= 1) & (p < UNITS + 1))
        def _():
            u = p - 1
            combine_mine(u)
            rs_copy(u, 0, 1).start()
            rs_copy(u, 1, 1).start()

        @pl.when((p >= 2) & (p < UNITS + 2))
        def _():
            rs_next(p - 2, 3)

        @pl.when((p >= 1) & (p < UNITS + 1))
        def _():
            rs_next(p - 1, 2)

        @pl.when((p >= 2) & (p < UNITS + 2))
        def _():
            rs_next(p - 2, 4)

        @pl.when(p >= 3)
        def _():
            u = p - 3
            rs_copy(u, 0, 4).wait_recv()
            rs_copy(u, 1, 4).wait_recv()
            acc[0, pl.ds(pl.multiple_of(u * TOK, TOK), TOK), 0:FU] = (
                ag[1, u, 0].astype(F32)
                + rsrecv[u, 0, 3].astype(F32)
                + rsrecv[u, 1, 3].astype(F32)
            )

        @pl.when(p == UNITS - 1)
        def _():
            by_owner = owner_ref[...] * dots[...]
            for j in range(NZ):
                dbuf[j] = lax.dot_general(
                    by_owner, sel[:, j * TOK : (j + 1) * TOK].astype(F32),
                    (((0,), (0,)), ((), ())),
                    preferred_element_type=F32, precision=lax.Precision.HIGHEST,
                )

            @pl.loop(1, NZ)
            def _(d):
                dots_copy(d).start()

    drx[0] = dbuf[0]

    @pl.loop(1, NZ)
    def _(d):
        dots_copy(d).wait_recv()

    ids_t = meta[0, 0:TOP]
    rows = []
    for k in range(TOP):
        got = jnp.zeros((PLANE, TOK), F32)
        for m in range(NZ):
            plane = z + m
            plane = jnp.where(plane >= NZ, plane - NZ, plane)
            got = got + jnp.where(ids_t[k : k + 1, :] == experts_of(plane), drx[m], 0.0)
        rows.append(jnp.sum(got, axis=0, keepdims=True))
    ggx[0] = jnp.concatenate(rows, axis=0)
    gg_copy = rc(ggx.at[0], ggx.at[1], es.at[0], er.at[0], sib)
    gg_copy.start()

    values = first_ref[...].astype(F32)
    inverse = lax.rsqrt(jnp.mean(values * values, axis=1, keepdims=True) + EPSILON)
    total = jnp.concatenate([acc[0, u * TOK : (u + 1) * TOK, 0:FU] for u in range(UNITS)], axis=1)

    @pl.when(r == 0)
    def _():
        obuf[...] = (second_ref[...].astype(F32) - total).astype(BF)

    @pl.when(r == 1)
    def _():
        grad = total * gain_ref[...].astype(F32)
        obuf[...] = (
            inverse * grad
            - values * inverse * inverse * inverse * jnp.mean(grad * values, axis=1, keepdims=True)
        ).astype(BF)

    out_copy = rc(obuf, orecv, es.at[1], er.at[1], sib)
    out_copy.start()

    @pl.loop(0, UNITS)
    def _(u):
        @pl.loop(1, PLANE)
        def _(n):
            ret_copy(u, n).wait_send()

        for step in range(1, 5):
            rs_copy(u, 0, step).wait_send()
            rs_copy(u, 1, step).wait_send()
        t_copy(u).wait_send()
        wd_out(u).wait()

    @pl.loop(1, NZ)
    def _(d):
        dots_copy(d).wait_send()
        meta_copy(d).wait_send()

    gg_copy.wait()
    gg_ref[...] = ggx[0] + ggx[1]
    out_copy.wait()

    @pl.when(r == 0)
    def _():
        inv_ref[...] = obuf[...]
        fg_ref[...] = orecv[...]

    @pl.when(r == 1)
    def _():
        inv_ref[...] = orecv[...]
        fg_ref[...] = obuf[...]


def slot_tables():
    slot = np.arange(ROWS)
    owner = (slot[:, None] // SEG == np.arange(PLANE)[None, :]).astype(np.float32)
    block, order = slot % SEG // SHARE, slot % SHARE
    rank = np.where(block[:, None] == np.arange(NZ)[None, :], order[:, None], -100)
    return owner, rank.astype(np.float32)


def local(first, second, cot, gain, ids, gates, w_gate, w_up, w_down):
    owner, rank = slot_tables()
    vmem = pl.BlockSpec(memory_space=pltpu.VMEM)
    hbm = pl.BlockSpec(memory_space=pl.ANY)
    dma = pltpu.SemaphoreType.DMA
    inv, fg, gg, wdg = pl.pallas_call(
        kernel,
        out_shape=(
            jax.ShapeDtypeStruct((TOK, WIDTH), BF),
            jax.ShapeDtypeStruct((TOK, WIDTH), BF),
            jax.ShapeDtypeStruct((TOP, TOK), F32),
            jax.ShapeDtypeStruct((HALF, WIDTH), BF),
        ),
        in_specs=[vmem] * 8 + [hbm] * 3,
        out_specs=(vmem, vmem, vmem, hbm),
        scratch_shapes=[
            pltpu.VMEM((WIDTH, FF), BF),
            pltpu.VMEM((WIDTH, FF), BF),
            pltpu.VMEM((FF, WIDTH), BF),
            pltpu.VMEM((2, UNITS, NZ, TOK, FU), BF),
            pltpu.VMEM((NZ, 2 * TOP, TOK), F32),
            pltpu.VMEM((ROWS, NZ * TOK), BF),
            pltpu.VMEM((NZ * TOK, ROWS), BF),
            pltpu.VMEM((ROWS, 1), F32),
            pltpu.VMEM((UNITS, ROWS, FU), BF),
            pltpu.VMEM((UNITS, PLANE, SEG, 2 * FU), BF),
            pltpu.VMEM((UNITS, PLANE, SEG, 2 * FU), BF),
            pltpu.VMEM((UNITS, PLANE, SEG, 2 * FU), BF),
            pltpu.VMEM((3, ROWS, FF), F32),
            pltpu.VMEM((ROWS, FF), BF),
            pltpu.VMEM((ROWS, FF), BF),
            pltpu.VMEM((ROWS, FF), BF),
            pltpu.VMEM((UNITS, 2, 4, TOK, FU), BF),
            pltpu.VMEM((UNITS, HALF, FU), BF),
            pltpu.VMEM((UNITS, HALF, FU), BF),
            pltpu.VMEM((ROWS, 1), F32),
            pltpu.VMEM((NZ, PLANE, TOK), F32),
            pltpu.VMEM((NZ, PLANE, TOK), F32),
            pltpu.VMEM((2, TOP, TOK), F32),
            pltpu.VMEM((TOK, WIDTH), BF),
            pltpu.VMEM((TOK, WIDTH), BF),
            dma((3,)), dma((3,)), dma((3,)),
            dma((UNITS, 2, 4)), dma((UNITS, 2, 4)),
            dma((UNITS, NZ)), dma((UNITS, NZ)),
            dma((NZ,)), dma((NZ,)),
            dma((UNITS, PLANE)), dma((UNITS, PLANE)),
            dma((UNITS, PLANE)), dma((UNITS, PLANE)),
            dma((UNITS,)), dma((UNITS,)),
            dma((UNITS, 2, 4)), dma((UNITS, 2, 4)),
            dma((UNITS,)), dma((UNITS,)),
            dma((NZ,)), dma((NZ,)),
            dma((2,)), dma((2,)), dma((UNITS,)), pltpu.SemaphoreType.REGULAR,
        ],
        compiler_params=pltpu.CompilerParams(
            collective_id=1, has_side_effects=True, vmem_limit_bytes=63 << 20
        ),
        name="experts_backward",
    )(
        first, second, cot, gain.reshape(1, WIDTH), ids, gates.T,
        jnp.asarray(owner), jnp.asarray(rank), w_gate[0], w_up[0], w_down[0],
    )
    return inv, fg, gg.T, wdg[None]


def solution(mesh):
    rows = P("ep", None)
    return jax.shard_map(
        local,
        mesh=mesh,
        in_specs=(
            rows, rows, rows, P(), rows, rows,
            P("ep", None, "rep"), P("ep", None, "rep"), P("ep", "rep", None),
        ),
        out_specs=(rows, rows, rows, P("ep", "rep", None)),
        check_vma=False,
    )
```

time: 628 us -> 233 us (0.37); the launches traced: 615 us -> 233 us
  Pallas kernels: 0 us -> 224 us
  blocking collectives: 207 us -> 0 us
  waiting for transfers between devices: 179 us -> 0 us
  local copies, waits for them, and re-layouts: 117 us -> 8.33 us
  matrix products: 40.9 us -> 0 us
  starting transfers between devices: 29 us -> 0 us
  other arithmetic: 27.4 us -> 0 us
  between operations: 14.8 us -> 0.66 us
    pallas_call x0 -> x1, Pallas kernels: none -> 224 us  [local(): pl.pallas_call(kernel, out_shape=(jax.ShapeDtypeStruct((TOK, WIDTH), BF),...]
    all_to_all x2 -> x0, blocking collectives: 207 us -> none  [the longest x1 104 us: local(): lax.all_to_all(back_grad, 'ep', split_axis=0, concat_axis=0, tiled=True)]
    all_to_all x2 -> x0, waiting for transfers between devices: 177 us -> none  [the longest x1 92 us: local(): lax.all_to_all(mine_inputs, 'ep', split_axis=0, concat_axis=0, tiled=True)]
    dot_general x9 -> x0, matrix products: 40.9 us -> none  [the longest x3 10.9 us: contract_cols(): lax.dot_general(left, right, (((1,), (1,)), ((), ())), preferred_element_...]
    gather x6 -> x0, local copies, waits for them, and re-layouts: 39.9 us -> none  [the longest x1 12.2 us: local(): out_rows = whole_out[target].reshape(token_count, top_count, model_width)]
    all_to_all x2 -> x0, starting transfers between devices: 28.1 us -> none  [the longest x1 16.9 us: local(): lax.all_to_all(mine_inputs, 'ep', split_axis=0, concat_axis=0, tiled=True)]
    all_to_all x6 -> x0, local copies, waits for them, and re-layouts: 27.2 us -> none  [the longest x2 8.77 us: local(): lax.all_to_all(back_out, 'ep', split_axis=0, concat_axis=0, tiled=True)]
    reshape x3 -> x1, local copies, waits for them, and re-layouts: 20.5 us -> 1.29 us  [local(): gain.reshape(1, WIDTH)]
  transfers between devices with their start and end apart: 8 -> 0, of which waited for: 2 -> 0; matrix products, arithmetic and copies ran while one was open for 18% -> 0% of each run, Pallas kernels for 0% -> 0%
where the time goes in v1:
time: 233 us
  Pallas kernels  224 us (96%)
  local copies, waits for them, and re-layouts  8.33 us (4%)
    pallas_call x1, Pallas kernels, local(): pl.pallas_call(kernel, out_shape=(jax.ShapeDtypeStruct((TOK, WIDTH), BF),...  224 us
    unnamed x9, local copies, waits for them, and re-layouts  7.04 us

profile of v1, /device:TPU:1, one launch (start us, length us, event | category | flops | bytes accessed | tf_op | source)
XLA Modules:
  0.0 232.9 jit_solution(16237752991959099885)
XLA Ops:
  0.6 1.3 reshape.11.gain_ref
  1.9 1.4 copy.15.ids_ref
  3.3 223.9 %experts_backward.1 = (bf16[128,2048]{1,0:T(8,128)(2,1)}, bf16[128,2048]{1,0:T(8,128)(2,1)}, f32[8,128]{1,0:T(8,128)}, bf16[384,2048]{1,0:T(8,128)(2,1)}) custom-call(bf16[128,2048]{1,0:T(8,128)(2,1)} %first_ref.1, bf16[128,2048]{1,0:T(8,128)(2,1)} %second_ref.1, bf16[128,2048]{1,0:T(8,128)(2,1)} %cot_ref.1, bf16[1,2048]{1,0:T(2,128)(2,1)} %reshape.11.gain_ref, ...), custom_call_target="tpu_custom_call" | custom-call | tf_op jit(solution)/shard_map/experts_backward/pallas_call | solution.py:549
  227.3 0.0 copy-start.1
  227.3 0.0 copy-start
  227.3 2.0 copy.20
  229.3 1.9 copy.21
  231.2 0.0 copy-done.1
  231.2 0.6 copy.22
  231.8 0.0 copy-done
  231.8 1.1 copy.23
Async XLA Ops:
  227.3 3.9 %copy-start.1 = (f32[8,128]{1,0:T(8,128)S(1)}, f32[8,128]{1,0:T(8,128)}, u32[]{:S(2)}) copy-start(f32[8,128]{1,0:T(8,128)} %get-tuple-element.10) | copy-start | bytes 12292
  227.3 4.5 %copy-start = (bf16[384,2048]{1,0:T(8,128)(2,1)S(1)}, bf16[384,2048]{1,0:T(8,128)(2,1)}, u32[]{:S(2)}) copy-start(bf16[384,2048]{1,0:T(8,128)(2,1)} %get-tuple-element.11) | copy-start | bytes 4718596

commit v2 on v1

--- a/solution.py
+++ b/solution.py
@@ -21,11 +21,14 @@
 SHARE = 5
 SEG = NZ * SHARE
 ROWS = PLANE * SEG
-UNITS = 4
+UNITS = 8
 FU = WIDTH // UNITS
 HU = FU // 2
 PARTS = 2
 PROWS, PCHIPS = ROWS // PARTS, PLANE // PARTS
+AHEAD = 3
+ORDER = (10, 6, 14, 9, 11, 5, 7, 13, 15, 2, 8, 1, 4, 3, 12)
+LAG = 3
 PTOK, PBLK = NZ * TOK // PARTS, NZ // PARTS
 
 
@@ -42,13 +45,13 @@
 
 
 def kernel(
-    first_ref, second_ref, cot_ref, gain_ref, ids_ref, gates_ref, owner_ref, rank_ref,
+    first_ref, cot_ref, gain_ref, ids_ref, gates_ref, owner_ref, rank_ref,
     wg_hbm, wu_hbm, wd_hbm,
-    inv_ref, fg_ref, gg_ref, wdg_hbm,
+    tot_hbm, gg_ref, wdg_hbm,
     wg, wu, wd, ag, meta, sel, selt, gslot, sgsel, sbuf, drecv, rrecv, acc, hid, ggr, ugr,
-    rsrecv, wsend, wrecv, dots, dbuf, drx, ggx, obuf, orecv,
+    rsrecv, wsend, wrecv, dots, dbuf, drx, ggx,
     wl_sem, wss, wrs, ags, agr, sbs, sbr, ms, mr, dss, dsr, rss, rsr, ts, tr, qs, qr,
-    wgs, wgr, ds_, dr_, es, er, wos, free,
+    wgs, wgr, ds_, dr_, es, er, wos, tl, tss, trs, free,
 ):
     r = lax.axis_index("rep")
     ep = lax.axis_index("ep")
@@ -101,15 +104,7 @@
     for u in range(UNITS):
         ag[0, u, 0] = normed[:, u * FU : (u + 1) * FU]
         ag[1, u, 0] = cot_ref[:, u * FU : (u + 1) * FU]
-    eye = (
-        lax.broadcasted_iota(jnp.int32, (TOK, TOK), 0)
-        == lax.broadcasted_iota(jnp.int32, (TOK, TOK), 1)
-    ).astype(F32)
-    ids_t = lax.dot_general(
-        ids_ref[...].astype(F32), eye, (((0,), (0,)), ((), ())),
-        preferred_element_type=F32, precision=lax.Precision.HIGHEST,
-    )
-    meta[0, 0:TOP] = ids_t
+    meta[0, 0:TOP] = ids_ref[...].astype(F32)
     meta[0, TOP : 2 * TOP] = gates_ref[...]
 
     pl.semaphore_wait(barrier, NZ + PLANE - 1)
@@ -144,6 +139,11 @@
             sib_copy(u, j).start()
 
     ag_first(0)
+    ag_first(1)
+
+    sibling_weights()[0].start()
+    acc[...] = jnp.zeros_like(acc)
+    dots[...] = jnp.zeros_like(dots)
 
     def meta_copy(d):
         return rc(meta.at[0], meta.at[NZ - d], ms.at[d], mr.at[NZ - d], at(0, d, 0))
@@ -151,13 +151,6 @@
     @pl.loop(1, NZ)
     def _(d):
         meta_copy(d).start()
-
-    for copy in sibling_weights():
-        copy.start()
-
-    @pl.loop(1, NZ)
-    def _(d):
-        meta_copy(d).wait_recv()
 
     d_index = lax.broadcasted_iota(jnp.int32, (PLANE, 1), 0)
     dx, dy = d_index >> 2, d_index & 3
@@ -176,7 +169,10 @@
     gslot[...] = jnp.zeros_like(gslot)
     owner = owner_ref[...]
     first_rank = (r * SHARE).astype(F32)
-    for j in range(NZ):
+
+    def slots_of(j):
+        if j:
+            meta_copy(NZ - j).wait_recv()
         hits = jnp.zeros((PLANE, TOK), F32)
         weight = jnp.zeros((PLANE, TOK), F32)
         for k in range(TOP):
@@ -194,6 +190,21 @@
         sel[:, j * TOK : (j + 1) * TOK] = chosen.astype(BF)
         selt[j * TOK : (j + 1) * TOK, :] = chosen.T.astype(BF)
 
+    slots_of(0)
+    slots_of(1)
+    ag_next(0, 2)
+    slots_of(7)
+    slots_of(2)
+    ag_next(0, 3)
+    ag_next(1, 2)
+    slots_of(6)
+    slots_of(3)
+    ag_first(2)
+    ag_next(0, 4)
+    ag_next(1, 3)
+    slots_of(5)
+    slots_of(4)
+
     def back(n):
         i, j = n // NY, n % NY
         return ((NX - i) % NX) * NY + (NY - j) % NY
@@ -220,35 +231,117 @@
 
         drecv[u, 0] = sbuf[u, 0]
 
+        for n in ORDER:
+            disp_copy(u, n).start()
+
+    def wait_weights():
+        for copy in local_weights():
+            copy.wait()
+        for copy in sibling_weights():
+            copy.wait_send()
+        other = pl.ds(pl.multiple_of((1 - r) * HALF, 128), HALF)
+        rc(wg_hbm, wg.at[:, other], wss.at[0], wrs.at[0], sib).wait_recv()
+        rc(wu_hbm, wu.at[:, other], wss.at[1], wrs.at[1], sib).wait_recv()
+        rc(wd_hbm, wd.at[other, :], wss.at[2], wrs.at[2], sib).wait_recv()
+
+    def gather_rows(u):
         @pl.loop(1, PLANE)
         def _(n):
-            disp_copy(u, n).start()
-
-    @pl.loop(0, UNITS + 1)
-    def _(p):
-        u = p - 1
-
-        @pl.when((p >= 1) & (p < UNITS))
-        def _():
-            ag_first(p)
-
-        @pl.when(p >= 1)
-        def _():
-            ag_next(u, 3)
-
-        @pl.when(p < UNITS)
-        def _():
-            ag_next(p, 2)
-
-        @pl.when(p >= 1)
-        def _():
-            ag_next(u, 4)
-            ag_copy(u, 0, 4).wait_recv()
-            ag_copy(u, 1, 4).wait_recv()
-            sib_copy(u, 4).start()
-            for j in range(1, NZ):
-                sib_wait(u, j).wait_recv()
-            select(u)
+            disp_copy(u, n).wait_recv()
+
+    def project(u, c):
+        feats = pl.ds(pl.multiple_of(u * FU, FU), FU)
+        part = pl.ds(pl.multiple_of(c * PROWS, PROWS), PROWS)
+        chips = pl.ds(c * PCHIPS, PCHIPS)
+        rows = drecv[u, chips, :, 0:FU].reshape(PROWS, FU)
+        acc[0, part, :] += nn(rows, wg[feats, :])
+        acc[1, part, :] += nn(rows, wu[feats, :])
+        cots = drecv[u, chips, :, FU:].reshape(PROWS, FU)
+        acc[2, part, :] += nt(cots, wd[:, feats])
+
+    def project_all(u):
+        gather_rows(u)
+
+        @pl.loop(0, PARTS)
+        def _(c):
+            project(u, c)
+
+    def activate(c):
+        @pl.loop(0, PROWS // 80)
+        def _(k):
+            part = pl.ds(pl.multiple_of(c * PROWS + k * 80, 16), 80)
+            gate_pre, up_pre, grad = acc[0, part, :], acc[1, part, :], acc[2, part, :]
+            sig = jax.nn.sigmoid(gate_pre)
+            swish = gate_pre * sig
+            hid[part, :] = (swish * up_pre).astype(BF)
+            ggr[part, :] = (grad * up_pre * sig * (1.0 + gate_pre * (1.0 - sig))).astype(BF)
+            ugr[part, :] = (grad * swish).astype(BF)
+
+    def answer(u, c):
+        feats = pl.ds(pl.multiple_of(u * FU, FU), FU)
+        part = pl.ds(pl.multiple_of(c * PROWS, PROWS), PROWS)
+        chips = pl.ds(c * PCHIPS, PCHIPS)
+        outs = nn(hid[part, :], wd[:, feats]).astype(BF)
+        sbuf[u, chips, :, 0:FU] = outs.reshape(PCHIPS, SEG, FU)
+        grads = (nt(ggr[part, :], wg[feats, :]) + nt(ugr[part, :], wu[feats, :])).astype(BF)
+        sbuf[u, chips, :, FU:] = grads.reshape(PCHIPS, SEG, FU)
+
+        @pl.loop(0, PCHIPS)
+        def _(k):
+            n = (c + 1) * PCHIPS - 1 - k
+
+            @pl.when(n > 0)
+            def _():
+                ret_copy(u, n).start()
+
+    def answer_all(u):
+        @pl.loop(0, PARTS)
+        def _(c):
+            answer(u, c)
+
+        rrecv[u, 0] = sbuf[u, 0]
+
+    @pl.loop(0, UNITS)
+    def _(u):
+        @pl.when(u + 1 < UNITS)
+        def _():
+            ag_next(u + 1, 4)
+
+        ag_copy(u, 0, 4).wait_recv()
+        ag_copy(u, 1, 4).wait_recv()
+        sib_copy(u, 4).start()
+
+        @pl.when(u + 2 < UNITS)
+        def _():
+            ag_next(u + 2, 2)
+
+        for j in range(1, NZ):
+            sib_wait(u, j).wait_recv()
+        select(u)
+
+        @pl.when(u + 2 < UNITS)
+        def _():
+            ag_next(u + 2, 3)
+
+        @pl.when(u + 3 < UNITS)
+        def _():
+            ag_first(u + 3)
+
+        @pl.when(u == 0)
+        def _():
+            sibling_weights()[1].start()
+
+        @pl.when(u == 1)
+        def _():
+            sibling_weights()[2].start()
+
+        @pl.when(u == LAG)
+        def _():
+            wait_weights()
+
+        @pl.when(u >= LAG)
+        def _():
+            project_all(u - LAG)
 
     @pl.loop(0, UNITS)
     def _(u):
@@ -260,44 +353,9 @@
 
     pl.semaphore_signal(free, inc=1, device_id=sib, device_id_type=MESH)
 
-    for copy in local_weights():
-        copy.wait()
-    for copy in sibling_weights():
-        copy.wait_send()
-    other = pl.ds(pl.multiple_of((1 - r) * HALF, 128), HALF)
-    rc(wg_hbm, wg.at[:, other], wss.at[0], wrs.at[0], sib).wait_recv()
-    rc(wu_hbm, wu.at[:, other], wss.at[1], wrs.at[1], sib).wait_recv()
-    rc(wd_hbm, wd.at[other, :], wss.at[2], wrs.at[2], sib).wait_recv()
-
-    acc[...] = jnp.zeros_like(acc)
-
-    @pl.loop(0, UNITS)
+    @pl.loop(UNITS - LAG, UNITS - 1)
     def _(u):
-        @pl.loop(1, PLANE)
-        def _(n):
-            disp_copy(u, n).wait_recv()
-
-        feats = pl.ds(pl.multiple_of(u * FU, FU), FU)
-
-        @pl.loop(0, PARTS)
-        def _(c):
-            part = pl.ds(pl.multiple_of(c * PROWS, PROWS), PROWS)
-            chips = pl.ds(c * PCHIPS, PCHIPS)
-            rows = drecv[u, chips, :, 0:FU].reshape(PROWS, FU)
-            acc[0, part, :] += nn(rows, wg[feats, :])
-            acc[1, part, :] += nn(rows, wu[feats, :])
-            cots = drecv[u, chips, :, FU:].reshape(PROWS, FU)
-            acc[2, part, :] += nt(cots, wd[:, feats])
-
-    @pl.loop(0, ROWS // 80)
-    def _(c):
-        part = pl.ds(pl.multiple_of(c * 80, 16), 80)
-        gate_pre, up_pre, grad = acc[0, part, :], acc[1, part, :], acc[2, part, :]
-        sig = jax.nn.sigmoid(gate_pre)
-        swish = gate_pre * sig
-        hid[part, :] = (swish * up_pre).astype(BF)
-        ggr[part, :] = (grad * up_pre * sig * (1.0 + gate_pre * (1.0 - sig))).astype(BF)
-        ugr[part, :] = (grad * swish).astype(BF)
+        project_all(u)
 
     @pl.loop(0, UNITS)
     def _(u):
@@ -305,28 +363,24 @@
         def _(n):
             disp_copy(u, n).wait_send()
 
-        feats = pl.ds(pl.multiple_of(u * FU, FU), FU)
-
-        @pl.loop(0, PARTS)
-        def _(c):
-            part = pl.ds(pl.multiple_of(c * PROWS, PROWS), PROWS)
-            chips = pl.ds(c * PCHIPS, PCHIPS)
-            outs = nn(hid[part, :], wd[:, feats]).astype(BF)
-            sbuf[u, chips, :, 0:FU] = outs.reshape(PCHIPS, SEG, FU)
-            grads = (nt(ggr[part, :], wg[feats, :]) + nt(ugr[part, :], wu[feats, :])).astype(BF)
-            sbuf[u, chips, :, FU:] = grads.reshape(PCHIPS, SEG, FU)
-
-        rrecv[u, 0] = sbuf[u, 0]
-
-        @pl.loop(1, PLANE)
-        def _(n):
-            ret_copy(u, n).start()
+    gather_rows(UNITS - 1)
+
+    @pl.loop(0, PARTS)
+    def _(c):
+        project(UNITS - 1, c)
+        activate(c)
+        answer(0, c)
+
+    rrecv[0, 0] = sbuf[0, 0]
+
+    @pl.loop(1, AHEAD)
+    def _(u):
+        answer_all(u)
 
     def wd_copy(u):
         return rc(wsend.at[u], wrecv.at[u], wgs.at[u], wgr.at[u], sib)
 
-    @pl.loop(0, UNITS)
-    def _(u):
+    def wd_other(u):
         half = hid[:, pl.ds(pl.multiple_of((1 - r) * HALF, 128), HALF)]
         wsend[u] = tn(half, drecv[u, :, :, FU:].reshape(ROWS, FU)).astype(BF)
         wd_copy(u).start()
@@ -335,13 +389,10 @@
         feats = pl.ds(pl.multiple_of(u * FU, FU), FU)
         return pltpu.make_async_copy(wsend.at[u], wdg_hbm.at[:, feats], wos.at[u])
 
-    mine = pl.ds(pl.multiple_of(r * HALF, 128), HALF)
-
-    @pl.loop(0, UNITS)
-    def _(u):
-        feats = pl.ds(pl.multiple_of(u * FU, FU), FU)
-        part = tn(hid[:, mine], drecv[u, :, :, FU:].reshape(ROWS, FU))
-        rc(wsend.at[u], wrecv.at[u], wgs.at[u], wgr.at[u], sib).wait_recv()
+    def wd_mine(u):
+        half = hid[:, pl.ds(pl.multiple_of(r * HALF, 128), HALF)]
+        part = tn(half, drecv[u, :, :, FU:].reshape(ROWS, FU))
+        wd_copy(u).wait_recv()
         wd_copy(u).wait_send()
         wsend[u] = (part + wrecv[u].astype(F32)).astype(BF)
         wd_out(u).start()
@@ -349,7 +400,6 @@
     def t_copy(u):
         return rc(ag.at[0, u], ag.at[1, u], ts.at[u], tr.at[u], sib)
 
-    dots[...] = jnp.zeros_like(dots)
     pl.semaphore_wait(free, 1)
 
     def combine_other(u):
@@ -413,11 +463,39 @@
     def dots_copy(d):
         return rc(dbuf.at[d], drx.at[NZ - d], ds_.at[d], dr_.at[NZ - d], at(0, d, 0))
 
-    @pl.loop(0, UNITS + 3)
+    def tot_part(u):
+        return acc.at[u % 2, pl.ds(pl.multiple_of(u // 2 * TOK, TOK), TOK), 0:FU]
+
+    def tot_copy(u):
+        return pltpu.make_async_copy(tot_part(u), tot_hbm.at[r, u], tl.at[u])
+
+    def tot_send(u):
+        return rc(tot_part(u), tot_hbm.at[r, u], tss.at[u], trs.at[u], sib)
+
+    def tot_wait(u):
+        return rc(tot_part(u), tot_hbm.at[1 - r, u], tss.at[u], trs.at[u], sib)
+
+    gg_copy = rc(ggx.at[0], ggx.at[1], es.at[0], er.at[0], sib)
+
+    @pl.loop(0, UNITS + 5)
     def _(p):
-        @pl.when(p < UNITS)
-        def _():
-            combine_other(p)
+        @pl.when(p >= 5)
+        def _():
+            u = p - 5
+            rs_copy(u, 0, 4).wait_recv()
+            rs_copy(u, 1, 4).wait_recv()
+            acc[u % 2, pl.ds(pl.multiple_of(u // 2 * TOK, TOK), TOK), 0:FU] = (
+                ag[1, u, 0].astype(F32)
+                + rsrecv[u, 0, 3].astype(F32)
+                + rsrecv[u, 1, 3].astype(F32)
+            )
+            tot_copy(u).start()
+            tot_send(u).start()
+
+        for step in (4, 3, 2):
+            @pl.when((p >= step) & (p < UNITS + step))
+            def _(step=step):
+                rs_next(p - step, step)
 
         @pl.when((p >= 1) & (p < UNITS + 1))
         def _():
@@ -426,28 +504,21 @@
             rs_copy(u, 0, 1).start()
             rs_copy(u, 1, 1).start()
 
-        @pl.when((p >= 2) & (p < UNITS + 2))
-        def _():
-            rs_next(p - 2, 3)
+        @pl.when(p + AHEAD < UNITS)
+        def _():
+            answer_all(p + AHEAD)
+
+        @pl.when(p < UNITS)
+        def _():
+            wd_other(p)
 
         @pl.when((p >= 1) & (p < UNITS + 1))
         def _():
-            rs_next(p - 1, 2)
-
-        @pl.when((p >= 2) & (p < UNITS + 2))
-        def _():
-            rs_next(p - 2, 4)
-
-        @pl.when(p >= 3)
-        def _():
-            u = p - 3
-            rs_copy(u, 0, 4).wait_recv()
-            rs_copy(u, 1, 4).wait_recv()
-            acc[0, pl.ds(pl.multiple_of(u * TOK, TOK), TOK), 0:FU] = (
-                ag[1, u, 0].astype(F32)
-                + rsrecv[u, 0, 3].astype(F32)
-                + rsrecv[u, 1, 3].astype(F32)
-            )
+            wd_mine(p - 1)
+
+        @pl.when(p < UNITS)
+        def _():
+            combine_other(p)
 
         @pl.when(p == UNITS - 1)
         def _():
@@ -463,43 +534,25 @@
             def _(d):
                 dots_copy(d).start()
 
-    drx[0] = dbuf[0]
-
-    @pl.loop(1, NZ)
-    def _(d):
-        dots_copy(d).wait_recv()
-
-    ids_t = meta[0, 0:TOP]
-    rows = []
-    for k in range(TOP):
-        got = jnp.zeros((PLANE, TOK), F32)
-        for m in range(NZ):
-            plane = z + m
-            plane = jnp.where(plane >= NZ, plane - NZ, plane)
-            got = got + jnp.where(ids_t[k : k + 1, :] == experts_of(plane), drx[m], 0.0)
-        rows.append(jnp.sum(got, axis=0, keepdims=True))
-    ggx[0] = jnp.concatenate(rows, axis=0)
-    gg_copy = rc(ggx.at[0], ggx.at[1], es.at[0], er.at[0], sib)
-    gg_copy.start()
-
-    values = first_ref[...].astype(F32)
-    inverse = lax.rsqrt(jnp.mean(values * values, axis=1, keepdims=True) + EPSILON)
-    total = jnp.concatenate([acc[0, u * TOK : (u + 1) * TOK, 0:FU] for u in range(UNITS)], axis=1)
-
-    @pl.when(r == 0)
-    def _():
-        obuf[...] = (second_ref[...].astype(F32) - total).astype(BF)
-
-    @pl.when(r == 1)
-    def _():
-        grad = total * gain_ref[...].astype(F32)
-        obuf[...] = (
-            inverse * grad
-            - values * inverse * inverse * inverse * jnp.mean(grad * values, axis=1, keepdims=True)
-        ).astype(BF)
-
-    out_copy = rc(obuf, orecv, es.at[1], er.at[1], sib)
-    out_copy.start()
+        @pl.when(p == UNITS + 2)
+        def _():
+            drx[0] = dbuf[0]
+
+            @pl.loop(1, NZ)
+            def _(d):
+                dots_copy(d).wait_recv()
+
+            ids_t = meta[0, 0:TOP]
+            rows = []
+            for k in range(TOP):
+                got = jnp.zeros((PLANE, TOK), F32)
+                for m in range(NZ):
+                    plane = z + m
+                    plane = jnp.where(plane >= NZ, plane - NZ, plane)
+                    got = got + jnp.where(ids_t[k : k + 1, :] == experts_of(plane), drx[m], 0.0)
+                rows.append(jnp.sum(got, axis=0, keepdims=True))
+            ggx[0] = jnp.concatenate(rows, axis=0)
+            gg_copy.start()
 
     @pl.loop(0, UNITS)
     def _(u):
@@ -512,6 +565,9 @@
             rs_copy(u, 1, step).wait_send()
         t_copy(u).wait_send()
         wd_out(u).wait()
+        tot_copy(u).wait()
+        tot_send(u).wait_send()
+        tot_wait(u).wait_recv()
 
     @pl.loop(1, NZ)
     def _(d):
@@ -520,17 +576,30 @@
 
     gg_copy.wait()
     gg_ref[...] = ggx[0] + ggx[1]
-    out_copy.wait()
-
-    @pl.when(r == 0)
-    def _():
-        inv_ref[...] = obuf[...]
-        fg_ref[...] = orecv[...]
-
-    @pl.when(r == 1)
-    def _():
-        inv_ref[...] = orecv[...]
-        fg_ref[...] = obuf[...]
+
+
+def finish(
+    tot, first_ref, second_ref, gain_ref, gates_in, wd_in,
+    inv_ref, fg_ref, gg_ref, wd_ref, sem,
+):
+    copy = pltpu.make_async_copy(wd_in, wd_ref, sem)
+    copy.start()
+    gg_ref[...] = gates_in[...]
+    values = first_ref[...].astype(F32)
+    inverse = lax.rsqrt(jnp.mean(values * values, axis=1, keepdims=True) + EPSILON)
+    gain = gain_ref[...].astype(F32)
+    along = jnp.zeros((TOK, 1), F32)
+    for u in range(UNITS):
+        cols = slice(u * FU, (u + 1) * FU)
+        inv_ref[:, cols] = (second_ref[:, cols].astype(F32) - tot[0, u]).astype(BF)
+        along = along + jnp.sum(tot[1, u] * gain[:, cols] * values[:, cols], axis=1, keepdims=True)
+    shift = inverse * inverse * inverse * (along / WIDTH)
+    for u in range(UNITS):
+        cols = slice(u * FU, (u + 1) * FU)
+        fg_ref[:, cols] = (
+            inverse * (tot[1, u] * gain[:, cols]) - values[:, cols] * shift
+        ).astype(BF)
+    copy.wait()
 
 
 def slot_tables():
@@ -546,16 +615,16 @@
     vmem = pl.BlockSpec(memory_space=pltpu.VMEM)
     hbm = pl.BlockSpec(memory_space=pl.ANY)
     dma = pltpu.SemaphoreType.DMA
-    inv, fg, gg, wdg = pl.pallas_call(
+    gain = gain.reshape(1, WIDTH)
+    tot, gg, wdg = pl.pallas_call(
         kernel,
         out_shape=(
-            jax.ShapeDtypeStruct((TOK, WIDTH), BF),
-            jax.ShapeDtypeStruct((TOK, WIDTH), BF),
+            jax.ShapeDtypeStruct((2, UNITS, TOK, FU), F32),
             jax.ShapeDtypeStruct((TOP, TOK), F32),
             jax.ShapeDtypeStruct((HALF, WIDTH), BF),
         ),
-        in_specs=[vmem] * 8 + [hbm] * 3,
-        out_specs=(vmem, vmem, vmem, hbm),
+        in_specs=[vmem] * 7 + [hbm] * 3,
+        out_specs=(hbm, vmem, hbm),
         scratch_shapes=[
             pltpu.VMEM((WIDTH, FF), BF),
             pltpu.VMEM((WIDTH, FF), BF),
@@ -580,8 +649,6 @@
             pltpu.VMEM((NZ, PLANE, TOK), F32),
             pltpu.VMEM((NZ, PLANE, TOK), F32),
             pltpu.VMEM((2, TOP, TOK), F32),
-            pltpu.VMEM((TOK, WIDTH), BF),
-            pltpu.VMEM((TOK, WIDTH), BF),
             dma((3,)), dma((3,)), dma((3,)),
             dma((UNITS, 2, 4)), dma((UNITS, 2, 4)),
             dma((UNITS, NZ)), dma((UNITS, NZ)),
@@ -592,16 +659,31 @@
             dma((UNITS, 2, 4)), dma((UNITS, 2, 4)),
             dma((UNITS,)), dma((UNITS,)),
             dma((NZ,)), dma((NZ,)),
-            dma((2,)), dma((2,)), dma((UNITS,)), pltpu.SemaphoreType.REGULAR,
+            dma((1,)), dma((1,)), dma((UNITS,)),
+            dma((UNITS,)), dma((UNITS,)), dma((UNITS,)), pltpu.SemaphoreType.REGULAR,
         ],
         compiler_params=pltpu.CompilerParams(
             collective_id=1, has_side_effects=True, vmem_limit_bytes=63 << 20
         ),
         name="experts_backward",
     )(
-        first, second, cot, gain.reshape(1, WIDTH), ids, gates.T,
+        first, cot, gain, ids.T, gates.T,
         jnp.asarray(owner), jnp.asarray(rank), w_gate[0], w_up[0], w_down[0],
     )
+    inv, fg, gg, wdg = pl.pallas_call(
+        finish,
+        out_shape=(
+            jax.ShapeDtypeStruct((TOK, WIDTH), BF),
+            jax.ShapeDtypeStruct((TOK, WIDTH), BF),
+            jax.ShapeDtypeStruct((TOP, TOK), F32),
+            jax.ShapeDtypeStruct((HALF, WIDTH), BF),
+        ),
+        in_specs=[vmem] * 5 + [hbm],
+        out_specs=(vmem, vmem, vmem, hbm),
+        scratch_shapes=[dma(())],
+        compiler_params=pltpu.CompilerParams(vmem_limit_bytes=62 << 20),
+        name="streams",
+    )(tot, first, second, gain, gg, wdg)
     return inv, fg, gg.T, wdg[None]
 
 

time: 233 us -> 253 us (1.086)
  Pallas kernels: 224 us -> 250 us
  local copies, waits for them, and re-layouts: 8.33 us -> 1.29 us
    pallas_call x1 -> x2, Pallas kernels: 224 us -> 250 us  [the longest x1 198 us: local(): pl.pallas_call(kernel, out_shape=(jax.ShapeDtypeStruct((2, UNITS, TOK, FU...]
    unnamed x9 -> x0, local copies, waits for them, and re-layouts: 7.04 us -> none
where the time goes in v2:
time: 253 us; the launch traced here: 252 us
  Pallas kernels  250 us (99%)
    pallas_call x1, Pallas kernels, local(): pl.pallas_call(kernel, out_shape=(jax.ShapeDtypeStruct((2, UNITS, TOK, FU...  198 us
    pallas_call x1, Pallas kernels, local(): pl.pallas_call(finish, out_shape=(jax.ShapeDtypeStruct((TOK, WIDTH), BF),...  51.6 us

profile of v2, /device:TPU:1, one launch (start us, length us, event | category | flops | bytes accessed | tf_op | source)
XLA Modules:
  0.0 252.0 jit_solution(8100701061532877985)
XLA Ops:
  0.6 1.3 reshape.11.gain_ref
  1.9 198.3 %experts_backward.1 = (f32[2,8,128,256]{3,2,1,0:T(8,128)}, f32[8,128]{1,0:T(8,128)}, bf16[384,2048]{1,0:T(8,128)(2,1)}) custom-call(bf16[128,2048]{1,0:T(8,128)(2,1)} %first_ref.3, bf16[128,2048]{1,0:T(8,128)(2,1)} %cot_ref.1, bf16[1,2048]{1,0:T(2,128)(2,1)} %reshape.11.gain_ref, s32[8,128]{1,0:T(8,128)} %bitcast.10, f32[8,128]{1,0:T(8,128)} %bitcast.11, ...), custom_call_target="tpu_custom_call" | custom-call | tf_op jit(solution)/shard_map/experts_backward/pallas_call | solution.py:619
  200.3 51.6 %streams.1 = (bf16[128,2048]{1,0:T(8,128)(2,1)}, bf16[128,2048]{1,0:T(8,128)(2,1)}, f32[8,128]{1,0:T(8,128)}, bf16[384,2048]{1,0:T(8,128)(2,1)}) custom-call(f32[2,8,128,256]{3,2,1,0:T(8,128)} %get-tuple-element.11.tot, bf16[128,2048]{1,0:T(8,128)(2,1)} %first_ref.3, bf16[128,2048]{1,0:T(8,128)(2,1)} %second_ref.1, bf16[1,2048]{1,0:T(2,128)(2,1)} %reshape.11.gain_ref, ...), custom_call_target="tpu_custom_call" | custom-call | tf_op jit(solution)/shard_map/streams/pallas_call | solution.py:673

commit v3 on v2

--- a/solution.py
+++ b/solution.py
@@ -29,15 +29,10 @@
 AHEAD = 3
 ORDER = (10, 6, 14, 9, 11, 5, 7, 13, 15, 2, 8, 1, 4, 3, 12)
 LAG = 3
-PTOK, PBLK = NZ * TOK // PARTS, NZ // PARTS
 
 
 def nt(left, right):
     return lax.dot_general(left, right, (((1,), (1,)), ((), ())), preferred_element_type=F32)
-
-
-def tn(left, right):
-    return lax.dot_general(left, right, (((0,), (0,)), ((), ())), preferred_element_type=F32)
 
 
 def nn(left, right):
@@ -48,7 +43,7 @@
     first_ref, cot_ref, gain_ref, ids_ref, gates_ref, owner_ref, rank_ref,
     wg_hbm, wu_hbm, wd_hbm,
     tot_hbm, gg_ref, wdg_hbm,
-    wg, wu, wd, ag, meta, sel, selt, gslot, sgsel, sbuf, drecv, rrecv, acc, hid, ggr, ugr,
+    wg, wu, wd, ag, meta, sel, selt, gslot, sgsel, sbuf, drecv, rrecv, acc, hid, hidt, ggr, ugr,
     rsrecv, wsend, wrecv, dots, dbuf, drx, ggx,
     wl_sem, wss, wrs, ags, agr, sbs, sbr, ms, mr, dss, dsr, rss, rsr, ts, tr, qs, qr,
     wgs, wgr, ds_, dr_, es, er, wos, tl, tss, trs, free,
@@ -186,7 +181,9 @@
         slot_gate = jnp.dot(
             owner, weight, preferred_element_type=F32, precision=lax.Precision.HIGHEST
         )
-        gslot[...] += jnp.sum(chosen * slot_gate, axis=1, keepdims=True)
+        gslot[...] += jnp.broadcast_to(
+            jnp.sum(chosen * slot_gate, axis=1, keepdims=True), (ROWS, TOK)
+        )
         sel[:, j * TOK : (j + 1) * TOK] = chosen.astype(BF)
         selt[j * TOK : (j + 1) * TOK, :] = chosen.T.astype(BF)
 
@@ -217,18 +214,16 @@
         m = back(n)
         return rc(sbuf.at[u, n], rrecv.at[u, m], rss.at[u, n], rsr.at[u, m], at(n // NY, 0, n % NY))
 
+    def wide(lanes):
+        return jnp.concatenate([lanes] * (FU // TOK), axis=1)
+
     def select(u):
-        @pl.loop(0, PARTS)
-        def _(c):
-            part = pl.ds(pl.multiple_of(c * PROWS, PROWS), PROWS)
-            chips = pl.ds(c * PCHIPS, PCHIPS)
-            rows = nn(sel[part, :], ag[0, u].reshape(NZ * TOK, FU)).astype(BF)
-            sbuf[u, chips, :, 0:FU] = rows.reshape(PCHIPS, SEG, FU)
-            cots = nn(sel[part, :], ag[1, u].reshape(NZ * TOK, FU))
-            sgsel[u, part, :] = cots.astype(BF)
-            scaled = (cots * gslot[part, :]).astype(BF)
-            sbuf[u, chips, :, FU:] = scaled.reshape(PCHIPS, SEG, FU)
-
+        rows = nn(sel[...], ag[0, u].reshape(NZ * TOK, FU)).astype(BF)
+        sbuf[u, :, :, 0:FU] = rows.reshape(PLANE, SEG, FU)
+        cots = nn(sel[...], ag[1, u].reshape(NZ * TOK, FU))
+        sgsel[u] = cots.astype(BF)
+        scaled = (cots * wide(gslot[...])).astype(BF)
+        sbuf[u, :, :, FU:] = scaled.reshape(PLANE, SEG, FU)
         drecv[u, 0] = sbuf[u, 0]
 
         for n in ORDER:
@@ -249,22 +244,21 @@
         def _(n):
             disp_copy(u, n).wait_recv()
 
-    def project(u, c):
+    def project(u, c, parts):
+        size, count = ROWS // parts, PLANE // parts
         feats = pl.ds(pl.multiple_of(u * FU, FU), FU)
-        part = pl.ds(pl.multiple_of(c * PROWS, PROWS), PROWS)
-        chips = pl.ds(c * PCHIPS, PCHIPS)
-        rows = drecv[u, chips, :, 0:FU].reshape(PROWS, FU)
+        part = pl.ds(pl.multiple_of(c * size, size), size)
+        chips = pl.ds(c * count, count)
+        rows = drecv[u, chips, :, 0:FU].reshape(size, FU)
         acc[0, part, :] += nn(rows, wg[feats, :])
         acc[1, part, :] += nn(rows, wu[feats, :])
-        cots = drecv[u, chips, :, FU:].reshape(PROWS, FU)
+        cots = drecv[u, chips, :, FU:].reshape(size, FU)
         acc[2, part, :] += nt(cots, wd[:, feats])
 
     def project_all(u):
         gather_rows(u)
 
-        @pl.loop(0, PARTS)
-        def _(c):
-            project(u, c)
+        project(u, 0, 1)
 
     def activate(c):
         @pl.loop(0, PROWS // 80)
@@ -277,27 +271,26 @@
             ggr[part, :] = (grad * up_pre * sig * (1.0 + gate_pre * (1.0 - sig))).astype(BF)
             ugr[part, :] = (grad * swish).astype(BF)
 
-    def answer(u, c):
+    def answer(u, c, parts):
+        size, count = ROWS // parts, PLANE // parts
         feats = pl.ds(pl.multiple_of(u * FU, FU), FU)
-        part = pl.ds(pl.multiple_of(c * PROWS, PROWS), PROWS)
-        chips = pl.ds(c * PCHIPS, PCHIPS)
+        part = pl.ds(pl.multiple_of(c * size, size), size)
+        chips = pl.ds(c * count, count)
         outs = nn(hid[part, :], wd[:, feats]).astype(BF)
-        sbuf[u, chips, :, 0:FU] = outs.reshape(PCHIPS, SEG, FU)
+        sbuf[u, chips, :, 0:FU] = outs.reshape(count, SEG, FU)
         grads = (nt(ggr[part, :], wg[feats, :]) + nt(ugr[part, :], wu[feats, :])).astype(BF)
-        sbuf[u, chips, :, FU:] = grads.reshape(PCHIPS, SEG, FU)
-
-        @pl.loop(0, PCHIPS)
+        sbuf[u, chips, :, FU:] = grads.reshape(count, SEG, FU)
+
+        @pl.loop(0, count)
         def _(k):
-            n = (c + 1) * PCHIPS - 1 - k
+            n = (c + 1) * count - 1 - k
 
             @pl.when(n > 0)
             def _():
                 ret_copy(u, n).start()
 
     def answer_all(u):
-        @pl.loop(0, PARTS)
-        def _(c):
-            answer(u, c)
+        answer(u, 0, 1)
 
         rrecv[u, 0] = sbuf[u, 0]
 
@@ -367,9 +360,9 @@
 
     @pl.loop(0, PARTS)
     def _(c):
-        project(UNITS - 1, c)
+        project(UNITS - 1, c, PARTS)
         activate(c)
-        answer(0, c)
+        answer(0, c, PARTS)
 
     rrecv[0, 0] = sbuf[0, 0]
 
@@ -377,12 +370,16 @@
     def _(u):
         answer_all(u)
 
+    for k in range(FF // TOK):
+        cols = slice(k * TOK, (k + 1) * TOK)
+        hidt[cols, :] = hid[:, cols].astype(F32).T.astype(BF)
+
     def wd_copy(u):
         return rc(wsend.at[u], wrecv.at[u], wgs.at[u], wgr.at[u], sib)
 
     def wd_other(u):
-        half = hid[:, pl.ds(pl.multiple_of((1 - r) * HALF, 128), HALF)]
-        wsend[u] = tn(half, drecv[u, :, :, FU:].reshape(ROWS, FU)).astype(BF)
+        half = hidt[pl.ds(pl.multiple_of((1 - r) * HALF, HALF), HALF), :]
+        wsend[u] = nn(half, drecv[u, :, :, FU:].reshape(ROWS, FU)).astype(BF)
         wd_copy(u).start()
 
     def wd_out(u):
@@ -390,8 +387,8 @@
         return pltpu.make_async_copy(wsend.at[u], wdg_hbm.at[:, feats], wos.at[u])
 
     def wd_mine(u):
-        half = hid[:, pl.ds(pl.multiple_of(r * HALF, 128), HALF)]
-        part = tn(half, drecv[u, :, :, FU:].reshape(ROWS, FU))
+        half = hidt[pl.ds(pl.multiple_of(r * HALF, HALF), HALF), :]
+        part = nn(half, drecv[u, :, :, FU:].reshape(ROWS, FU))
         wd_copy(u).wait_recv()
         wd_copy(u).wait_send()
         wsend[u] = (part + wrecv[u].astype(F32)).astype(BF)
@@ -407,34 +404,23 @@
         def _(n):
             ret_copy(u, n).wait_recv()
 
-        @pl.loop(0, PARTS)
-        def _(c):
-            part = pl.ds(pl.multiple_of(c * PROWS, PROWS), PROWS)
-            chips = pl.ds(c * PCHIPS, PCHIPS)
-            outs = rrecv[u, chips, :, 0:FU].astype(F32).reshape(PROWS, FU)
-            dots[part, :] += jnp.sum(outs * sgsel[u, part, :].astype(F32), axis=1, keepdims=True)
-            rrecv[u, chips, :, 0:FU] = (outs * gslot[part, :]).astype(BF).reshape(PCHIPS, SEG, FU)
+        outs = rrecv[u, :, :, 0:FU].astype(F32).reshape(ROWS, FU)
+        terms = outs * sgsel[u].astype(F32)
+        for k in range(FU // TOK):
+            dots[...] += terms[:, k * TOK : (k + 1) * TOK]
+        rrecv[u, :, :, 0:FU] = (outs * wide(gslot[...])).astype(BF).reshape(PLANE, SEG, FU)
 
         kept = rrecv[u, :, :, pl.ds(pl.multiple_of((1 - r) * FU, FU), FU)].reshape(ROWS, FU)
 
-        @pl.loop(0, PARTS)
-        def _(c):
-            part = pl.ds(pl.multiple_of(c * PTOK, PTOK), PTOK)
-            blocks = pl.ds(c * PBLK, PBLK)
-            ag[0, u, blocks] = nn(selt[part, :], kept).astype(BF).reshape(PBLK, TOK, FU)
-
+        ag[0, u] = nn(selt[...], kept).astype(BF).reshape(NZ, TOK, FU)
         t_copy(u).start()
 
     def combine_mine(u):
         t_copy(u).wait_recv()
         kept = rrecv[u, :, :, pl.ds(pl.multiple_of(r * FU, FU), FU)].reshape(ROWS, FU)
 
-        @pl.loop(0, PARTS)
-        def _(c):
-            part = pl.ds(pl.multiple_of(c * PTOK, PTOK), PTOK)
-            blocks = pl.ds(c * PBLK, PBLK)
-            total = nn(selt[part, :], kept).reshape(PBLK, TOK, FU) + ag[1, u, blocks].astype(F32)
-            ag[1, u, blocks] = total.astype(BF)
+        total = nn(selt[...], kept).reshape(NZ, TOK, FU) + ag[1, u].astype(F32)
+        ag[1, u] = total.astype(BF)
 
     def rs_copy(u, way, step):
         sign = 1 - 2 * way
@@ -522,7 +508,7 @@
 
         @pl.when(p == UNITS - 1)
         def _():
-            by_owner = owner_ref[...] * dots[...]
+            by_owner = owner_ref[...] * jnp.sum(dots[...], axis=1, keepdims=True)
             for j in range(NZ):
                 dbuf[j] = lax.dot_general(
                     by_owner, sel[:, j * TOK : (j + 1) * TOK].astype(F32),
@@ -580,10 +566,9 @@
 
 def finish(
     tot, first_ref, second_ref, gain_ref, gates_in, wd_in,
-    inv_ref, fg_ref, gg_ref, wd_ref, sem,
+    inv_ref, fg_ref, gg_ref, wd_ref,
 ):
-    copy = pltpu.make_async_copy(wd_in, wd_ref, sem)
-    copy.start()
+    wd_ref[...] = wd_in[...]
     gg_ref[...] = gates_in[...]
     values = first_ref[...].astype(F32)
     inverse = lax.rsqrt(jnp.mean(values * values, axis=1, keepdims=True) + EPSILON)
@@ -599,7 +584,6 @@
         fg_ref[:, cols] = (
             inverse * (tot[1, u] * gain[:, cols]) - values[:, cols] * shift
         ).astype(BF)
-    copy.wait()
 
 
 def slot_tables():
@@ -633,19 +617,20 @@
             pltpu.VMEM((NZ, 2 * TOP, TOK), F32),
             pltpu.VMEM((ROWS, NZ * TOK), BF),
             pltpu.VMEM((NZ * TOK, ROWS), BF),
-            pltpu.VMEM((ROWS, 1), F32),
+            pltpu.VMEM((ROWS, TOK), F32),
             pltpu.VMEM((UNITS, ROWS, FU), BF),
             pltpu.VMEM((UNITS, PLANE, SEG, 2 * FU), BF),
             pltpu.VMEM((UNITS, PLANE, SEG, 2 * FU), BF),
             pltpu.VMEM((UNITS, PLANE, SEG, 2 * FU), BF),
             pltpu.VMEM((3, ROWS, FF), F32),
             pltpu.VMEM((ROWS, FF), BF),
+            pltpu.VMEM((FF, ROWS), BF),
             pltpu.VMEM((ROWS, FF), BF),
             pltpu.VMEM((ROWS, FF), BF),
             pltpu.VMEM((UNITS, 2, 4, TOK, FU), BF),
             pltpu.VMEM((UNITS, HALF, FU), BF),
             pltpu.VMEM((UNITS, HALF, FU), BF),
-            pltpu.VMEM((ROWS, 1), F32),
+            pltpu.VMEM((ROWS, TOK), F32),
             pltpu.VMEM((NZ, PLANE, TOK), F32),
             pltpu.VMEM((NZ, PLANE, TOK), F32),
             pltpu.VMEM((2, TOP, TOK), F32),
@@ -678,9 +663,8 @@
             jax.ShapeDtypeStruct((TOP, TOK), F32),
             jax.ShapeDtypeStruct((HALF, WIDTH), BF),
         ),
-        in_specs=[vmem] * 5 + [hbm],
-        out_specs=(vmem, vmem, vmem, hbm),
-        scratch_shapes=[dma(())],
+        in_specs=[vmem] * 6,
+        out_specs=(vmem,) * 4,
         compiler_params=pltpu.CompilerParams(vmem_limit_bytes=62 << 20),
         name="streams",
     )(tot, first, second, gain, gg, wdg)

time: 253 us -> 206 us (0.81)
  Pallas kernels: 250 us -> 202 us
    pallas_call x1, Pallas kernels: 51.6 us -> 4.31 us  [local(): pl.pallas_call(finish, out_shape=(jax.ShapeDtypeStruct((TOK, WIDTH), BF),...]
where the time goes in v3:
time: 206 us; the launch traced here: 204 us
  Pallas kernels  202 us (98%)
    pallas_call x1, Pallas kernels, local(): pl.pallas_call(kernel, out_shape=(jax.ShapeDtypeStruct((2, UNITS, TOK, FU...  198 us
    pallas_call x1, Pallas kernels, local(): pl.pallas_call(finish, out_shape=(jax.ShapeDtypeStruct((TOK, WIDTH), BF),...  4.31 us

profile of v3, /device:TPU:1, one launch (start us, length us, event | category | flops | bytes accessed | tf_op | source)
XLA Modules:
  0.0 204.3 jit_solution(18315479776491674493)
XLA Ops:
  0.6 1.3 reshape.11.gain_ref
  1.9 198.0 %experts_backward.1 = (f32[2,8,128,256]{3,2,1,0:T(8,128)}, f32[8,128]{1,0:T(8,128)}, bf16[384,2048]{1,0:T(8,128)(2,1)}) custom-call(bf16[128,2048]{1,0:T(8,128)(2,1)} %first_ref.3, bf16[128,2048]{1,0:T(8,128)(2,1)} %cot_ref.1, bf16[1,2048]{1,0:T(2,128)(2,1)} %reshape.11.gain_ref, s32[8,128]{1,0:T(8,128)} %bitcast.10, f32[8,128]{1,0:T(8,128)} %bitcast.11, ...), custom_call_target="tpu_custom_call" | custom-call | tf_op jit(solution)/shard_map/experts_backward/pallas_call | solution.py:603
  199.9 4.3 %streams.1 = (bf16[128,2048]{1,0:T(8,128)(2,1)}, bf16[128,2048]{1,0:T(8,128)(2,1)}, f32[8,128]{1,0:T(8,128)}, bf16[384,2048]{1,0:T(8,128)(2,1)}) custom-call(f32[2,8,128,256]{3,2,1,0:T(8,128)} %get-tuple-element.11.tot, bf16[128,2048]{1,0:T(8,128)(2,1)} %first_ref.3, bf16[128,2048]{1,0:T(8,128)(2,1)} %second_ref.1, bf16[1,2048]{1,0:T(2,128)(2,1)} %reshape.11.gain_ref, ...), custom_call_target="tpu_custom_call" | custom-call | tf_op jit(solution)/shard_map/streams/pallas_call | solution.py:658

commit v4 on v3

--- a/solution.py
+++ b/solution.py
@@ -134,11 +134,7 @@
             sib_copy(u, j).start()
 
     ag_first(0)
-    ag_first(1)
-
-    sibling_weights()[0].start()
-    acc[...] = jnp.zeros_like(acc)
-    dots[...] = jnp.zeros_like(dots)
+
 
     def meta_copy(d):
         return rc(meta.at[0], meta.at[NZ - d], ms.at[d], mr.at[NZ - d], at(0, d, 0))
@@ -146,6 +142,10 @@
     @pl.loop(1, NZ)
     def _(d):
         meta_copy(d).start()
+
+    ag_first(1)
+    sibling_weights()[0].start()
+    dots[...] = jnp.zeros_like(dots)
 
     d_index = lax.broadcasted_iota(jnp.int32, (PLANE, 1), 0)
     dx, dy = d_index >> 2, d_index & 3
@@ -187,20 +187,27 @@
         sel[:, j * TOK : (j + 1) * TOK] = chosen.astype(BF)
         selt[j * TOK : (j + 1) * TOK, :] = chosen.T.astype(BF)
 
+    def ag_last(u):
+        ag_copy(u, 0, 4).wait_recv()
+        ag_copy(u, 1, 4).wait_recv()
+        sib_copy(u, 4).start()
+
     slots_of(0)
+    ag_next(0, 2)
     slots_of(1)
-    ag_next(0, 2)
     slots_of(7)
-    slots_of(2)
     ag_next(0, 3)
     ag_next(1, 2)
+    slots_of(2)
     slots_of(6)
-    slots_of(3)
     ag_first(2)
     ag_next(0, 4)
     ag_next(1, 3)
+    slots_of(3)
     slots_of(5)
     slots_of(4)
+    acc[...] = jnp.zeros_like(acc)
+    ag_last(0)
 
     def back(n):
         i, j = n // NY, n % NY
@@ -296,45 +303,45 @@
 
     @pl.loop(0, UNITS)
     def _(u):
-        @pl.when(u + 1 < UNITS)
-        def _():
-            ag_next(u + 1, 4)
-
-        ag_copy(u, 0, 4).wait_recv()
-        ag_copy(u, 1, 4).wait_recv()
-        sib_copy(u, 4).start()
-
-        @pl.when(u + 2 < UNITS)
-        def _():
-            ag_next(u + 2, 2)
-
         for j in range(1, NZ):
             sib_wait(u, j).wait_recv()
         select(u)
 
+        @pl.when(u + 1 < UNITS)
+        def _():
+            ag_next(u + 1, 4)
+
         @pl.when(u + 2 < UNITS)
         def _():
+            ag_next(u + 2, 2)
+
+        @pl.when(u == 0)
+        def _():
+            sibling_weights()[1].start()
+
+        @pl.when(u == 1)
+        def _():
+            sibling_weights()[2].start()
+
+        @pl.when(u == LAG)
+        def _():
+            wait_weights()
+
+        @pl.when(u >= LAG)
+        def _():
+            project_all(u - LAG)
+
+        @pl.when(u + 1 < UNITS)
+        def _():
+            ag_last(u + 1)
+
+        @pl.when(u + 2 < UNITS)
+        def _():
             ag_next(u + 2, 3)
 
         @pl.when(u + 3 < UNITS)
         def _():
             ag_first(u + 3)
-
-        @pl.when(u == 0)
-        def _():
-            sibling_weights()[1].start()
-
-        @pl.when(u == 1)
-        def _():
-            sibling_weights()[2].start()
-
-        @pl.when(u == LAG)
-        def _():
-            wait_weights()
-
-        @pl.when(u >= LAG)
-        def _():
-            project_all(u - LAG)
 
     @pl.loop(0, UNITS)
     def _(u):
@@ -506,7 +513,7 @@
         def _():
             combine_other(p)
 
-        @pl.when(p == UNITS - 1)
+        @pl.when(p == UNITS)
         def _():
             by_owner = owner_ref[...] * jnp.sum(dots[...], axis=1, keepdims=True)
             for j in range(NZ):
@@ -520,7 +527,7 @@
             def _(d):
                 dots_copy(d).start()
 
-        @pl.when(p == UNITS + 2)
+        @pl.when(p == UNITS + 3)
         def _():
             drx[0] = dbuf[0]
 

time: 206 us -> 199 us (0.966)
  Pallas kernels: 202 us -> 194 us
    pallas_call x1, Pallas kernels: 198 us -> 190 us  [local(): pl.pallas_call(kernel, out_shape=(jax.ShapeDtypeStruct((2, UNITS, TOK, FU...]
where the time goes in v4:
time: 199 us; the launch traced here: 196 us
  Pallas kernels  194 us (97%)
    pallas_call x1, Pallas kernels, local(): pl.pallas_call(kernel, out_shape=(jax.ShapeDtypeStruct((2, UNITS, TOK, FU...  190 us
    pallas_call x1, Pallas kernels, local(): pl.pallas_call(finish, out_shape=(jax.ShapeDtypeStruct((TOK, WIDTH), BF),...  4.31 us

profile of v4, /device:TPU:1, one launch (start us, length us, event | category | flops | bytes accessed | tf_op | source)
XLA Modules:
  0.0 196.2 jit_solution(12342099548758846441)
XLA Ops:
  0.6 1.3 reshape.11.gain_ref
  1.9 190.0 %experts_backward.1 = (f32[2,8,128,256]{3,2,1,0:T(8,128)}, f32[8,128]{1,0:T(8,128)}, bf16[384,2048]{1,0:T(8,128)(2,1)}) custom-call(bf16[128,2048]{1,0:T(8,128)(2,1)} %first_ref.3, bf16[128,2048]{1,0:T(8,128)(2,1)} %cot_ref.1, bf16[1,2048]{1,0:T(2,128)(2,1)} %reshape.11.gain_ref, s32[8,128]{1,0:T(8,128)} %bitcast.10, f32[8,128]{1,0:T(8,128)} %bitcast.11, ...), custom_call_target="tpu_custom_call" | custom-call | tf_op jit(solution)/shard_map/experts_backward/pallas_call | solution.py:610
  191.9 4.3 %streams.1 = (bf16[128,2048]{1,0:T(8,128)(2,1)}, bf16[128,2048]{1,0:T(8,128)(2,1)}, f32[8,128]{1,0:T(8,128)}, bf16[384,2048]{1,0:T(8,128)(2,1)}) custom-call(f32[2,8,128,256]{3,2,1,0:T(8,128)} %get-tuple-element.11.tot, bf16[128,2048]{1,0:T(8,128)(2,1)} %first_ref.3, bf16[128,2048]{1,0:T(8,128)(2,1)} %second_ref.1, bf16[1,2048]{1,0:T(2,128)(2,1)} %reshape.11.gain_ref, ...), custom_call_target="tpu_custom_call" | custom-call | tf_op jit(solution)/shard_map/streams/pallas_call | solution.py:665

commit v5 on v4

--- a/solution.py
+++ b/solution.py
@@ -95,7 +95,7 @@
 
     values = first_ref[...].astype(F32)
     inverse = lax.rsqrt(jnp.mean(values * values, axis=1, keepdims=True) + EPSILON)
-    normed = (values * inverse * gain_ref[...].astype(F32)).astype(BF)
+    normed = (values * inverse * gain_ref[...].astype(F32).reshape(1, WIDTH)).astype(BF)
     for u in range(UNITS):
         ag[0, u, 0] = normed[:, u * FU : (u + 1) * FU]
         ag[1, u, 0] = cot_ref[:, u * FU : (u + 1) * FU]
@@ -116,11 +116,15 @@
             ags.at[u, way, step - 1], agr.at[u, way, step - 1], at(0, sign, 0),
         )
 
-    def sib_copy(u, j):
-        return rc(ag.at[r, u, j], ag.at[r, u, j], sbs.at[u, j], sbr.at[u, j], sib)
-
-    def sib_wait(u, j):
-        return rc(ag.at[1 - r, u, j], ag.at[1 - r, u, j], sbs.at[u, j], sbr.at[u, j], sib)
+    runs = (pl.ds(1, 3), pl.ds(5, 3), pl.ds(4, 1))
+
+    def sib_copy(u, k):
+        part = ag.at[r, u, runs[k]]
+        return rc(part, part, sbs.at[u, k], sbr.at[u, k], sib)
+
+    def sib_wait(u, k):
+        part = ag.at[1 - r, u, runs[k]]
+        return rc(part, part, sbs.at[u, k], sbr.at[u, k], sib)
 
     def ag_first(u):
         ag_copy(u, 0, 1).start()
@@ -130,8 +134,9 @@
         for way in range(2):
             ag_copy(u, way, step - 1).wait_recv()
             ag_copy(u, way, step).start()
-        for j in (NZ - (step - 1), step - 1):
-            sib_copy(u, j).start()
+        if step == 4:
+            sib_copy(u, 0).start()
+            sib_copy(u, 1).start()
 
     ag_first(0)
 
@@ -190,7 +195,7 @@
     def ag_last(u):
         ag_copy(u, 0, 4).wait_recv()
         ag_copy(u, 1, 4).wait_recv()
-        sib_copy(u, 4).start()
+        sib_copy(u, 2).start()
 
     slots_of(0)
     ag_next(0, 2)
@@ -303,8 +308,8 @@
 
     @pl.loop(0, UNITS)
     def _(u):
-        for j in range(1, NZ):
-            sib_wait(u, j).wait_recv()
+        for k in range(3):
+            sib_wait(u, k).wait_recv()
         select(u)
 
         @pl.when(u + 1 < UNITS)
@@ -348,8 +353,8 @@
         for step in range(1, 5):
             ag_copy(u, 0, step).wait_send()
             ag_copy(u, 1, step).wait_send()
-        for j in range(1, NZ):
-            sib_copy(u, j).wait_send()
+        for k in range(3):
+            sib_copy(u, k).wait_send()
 
     pl.semaphore_signal(free, inc=1, device_id=sib, device_id_type=MESH)
 
@@ -579,7 +584,7 @@
     gg_ref[...] = gates_in[...]
     values = first_ref[...].astype(F32)
     inverse = lax.rsqrt(jnp.mean(values * values, axis=1, keepdims=True) + EPSILON)
-    gain = gain_ref[...].astype(F32)
+    gain = gain_ref[...].astype(F32).reshape(1, WIDTH)
     along = jnp.zeros((TOK, 1), F32)
     for u in range(UNITS):
         cols = slice(u * FU, (u + 1) * FU)
@@ -606,7 +611,6 @@
     vmem = pl.BlockSpec(memory_space=pltpu.VMEM)
     hbm = pl.BlockSpec(memory_space=pl.ANY)
     dma = pltpu.SemaphoreType.DMA
-    gain = gain.reshape(1, WIDTH)
     tot, gg, wdg = pl.pallas_call(
         kernel,
         out_shape=(
@@ -643,7 +647,7 @@
             pltpu.VMEM((2, TOP, TOK), F32),
             dma((3,)), dma((3,)), dma((3,)),
             dma((UNITS, 2, 4)), dma((UNITS, 2, 4)),
-            dma((UNITS, NZ)), dma((UNITS, NZ)),
+            dma((UNITS, 3)), dma((UNITS, 3)),
             dma((NZ,)), dma((NZ,)),
             dma((UNITS, PLANE)), dma((UNITS, PLANE)),
             dma((UNITS, PLANE)), dma((UNITS, PLANE)),

time: 199 us -> 197 us (0.990)
  no operation moved by 1% of the time
where the time goes in v5:
time: 197 us; the launch traced here: 195 us
  Pallas kernels  194 us (98%)
    pallas_call x1, Pallas kernels, local(): pl.pallas_call(kernel, out_shape=(jax.ShapeDtypeStruct((2, UNITS, TOK, FU...  190 us
    pallas_call x1, Pallas kernels, local(): pl.pallas_call(finish, out_shape=(jax.ShapeDtypeStruct((TOK, WIDTH), BF),...  4.32 us

profile of v5, /device:TPU:1, one launch (start us, length us, event | category | flops | bytes accessed | tf_op | source)
XLA Modules:
  0.0 195.0 jit_solution(16807668476432289260)
XLA Ops:
  0.6 190.0 %experts_backward.1 = (f32[2,8,128,256]{3,2,1,0:T(8,128)}, f32[8,128]{1,0:T(8,128)}, bf16[384,2048]{1,0:T(8,128)(2,1)}) custom-call(bf16[128,2048]{1,0:T(8,128)(2,1)} %first_ref.3, bf16[128,2048]{1,0:T(8,128)(2,1)} %cot_ref.1, bf16[2048]{0:T(1024)(128)(2,1)} %gain_ref.3, s32[8,128]{1,0:T(8,128)} %bitcast.10, f32[8,128]{1,0:T(8,128)} %bitcast.11, ...), custom_call_target="tpu_custom_call" | custom-call | tf_op jit(solution)/shard_map/experts_backward/pallas_call | solution.py:614
  190.7 4.3 %streams.1 = (bf16[128,2048]{1,0:T(8,128)(2,1)}, bf16[128,2048]{1,0:T(8,128)(2,1)}, f32[8,128]{1,0:T(8,128)}, bf16[384,2048]{1,0:T(8,128)(2,1)}) custom-call(f32[2,8,128,256]{3,2,1,0:T(8,128)} %get-tuple-element.11.tot, bf16[128,2048]{1,0:T(8,128)(2,1)} %first_ref.3, bf16[128,2048]{1,0:T(8,128)(2,1)} %second_ref.1, bf16[2048]{0:T(1024)(128)(2,1)} %gain_ref.3, ...), custom_call_target="tpu_custom_call" | custom-call | tf_op jit(solution)/shard_map/streams/pallas_call | solution.py:669
